TPU v7x, 128 devices: a whole 4x4x4 slice. The times are simulated.
128 devices in a mesh: pipe: 2 (over y_hi), dp: 16 (over x, y_lo, core), tensor: 4 (over z).
Axes of the slice: x: 4, y: 4 (y_hi: 2, y_lo: 2; y = y_hi * 2 + y_lo), z: 4, core: 2. Of those that a mesh axis runs over, the one named last changes fastest.
Arguments:
- tokens: float32 [3, 1280, 1024], P(None, 'dp'), may hold values from -6 to 6
- cotangent: float32 [3, 1280, 1024], P(None, 'dp'), may hold values from -6 to 6
- doc_lengths: int32 [3, 16, 3], P(None, 'dp'), may hold values from 1 to 60, 80 in all within a row
- live_mask: int32 [3, 1280], P(None, 'dp'), may hold values from 0 to 1, as said below
- norm_gains: float32 [2, 2, 1024], P('pipe'), may hold values from 0.5 to 1.5
- norm_biases: float32 [2, 2, 1024], P('pipe'), may hold values from -2 to 2
- query_key_value: bfloat16 [2, 1024, 3, 1024], P('pipe', None, None, 'tensor'), may hold values from -0.1875 to 0.1875
- query_value_bias: float32 [2, 2, 1024], P('pipe', None, 'tensor'), may hold values from -2 to 2
- output_weight: bfloat16 [2, 1024, 1024], P('pipe', 'tensor'), may hold values from -0.75 to 0.75
- output_biases: float32 [2, 2, 1024], P('pipe'), may hold values from -2 to 2
- expand_weight: bfloat16 [2, 1024, 4096], P('pipe', None, 'tensor'), may hold values from -0.1875 to 0.1875
- expand_bias: float32 [2, 4096], P('pipe', 'tensor'), may hold values from -2 to 2
- reduce_weight: bfloat16 [2, 4096, 1024], P('pipe', 'tensor'), may hold values from -0.125 to 0.125
Outputs:
- activations: float32 [2, 3, 1280, 1024], P('pipe', None, 'dp')
- input_grads: float32 [2, 3, 1280, 1024], P('pipe', None, 'dp')
- norm_gains_grad: float32 [2, 2, 1024], P('pipe')
- norm_biases_grad: float32 [2, 2, 1024], P('pipe')
- query_key_value_grad: float32 [2, 1024, 3, 1024], P('pipe', None, None, 'tensor')
- query_value_bias_grad: float32 [2, 2, 1024], P('pipe', None, 'tensor')
- output_weight_grad: float32 [2, 1024, 1024], P('pipe', 'tensor')
- output_biases_grad: float32 [2, 2, 1024], P('pipe')
- expand_weight_grad: float32 [2, 1024, 4096], P('pipe', None, 'tensor')
- expand_bias_grad: float32 [2, 4096], P('pipe', 'tensor')
- reduce_weight_grad: float32 [2, 4096, 1024], P('pipe', 'tensor')
Inputs may be any that keep to these rules, and one draw needn't show every extreme that they name: `live_mask`: in each slot of 80 tokens the live tokens form a prefix of at least 26 tokens; in every micro-batch some slot is fully live.
All inputs are finite; a program needn't handle non-finite values.
Results may differ from a plain program's by a relative error of at most 0.035.
Values may be sent and summed in bfloat16 or wider, within the bound.
A program may use at most 192 MiB of HBM per device.

v0:
```python
from functools import partial
import math

import jax
import jax.numpy as jnp
from jax import lax
from jax.sharding import PartitionSpec as P

HD = 64


def from_behind(block, axis, distance):
    devices = range(lax.axis_size(axis))
    route = [(i - distance, i) for i in devices if i - distance in devices]
    return lax.ppermute(block, axis, route)


def layer_norm(inputs, gain, shift):
    center = inputs - jnp.mean(inputs, -1, keepdims=True)
    spread = jnp.mean(center * center, -1, keepdims=True)
    return center * lax.rsqrt(spread + 1e-05) * gain + shift


def attention_mask(lengths, live):
    row_count = live.shape[0]
    ends = jnp.cumsum(lengths)
    places = jnp.arange(row_count, dtype=jnp.int32)
    segment = jnp.sum((places[:, None] >= ends[None, :]).astype(jnp.int32), 1)
    same = segment[:, None] == segment[None, :]
    causal = places[:, None] >= places[None, :]
    visible = (live[None, :] == 1) | (places[:, None] == places[None, :])
    return same & causal & visible


def score_block(queries, key_rows, allowed):
    row_count = queries.shape[0]
    query_heads = queries.reshape(row_count, -1, HD)
    key_heads = key_rows.reshape(row_count, -1, HD)
    raw_scores = jnp.einsum(
        "qhe,khe->hqk", query_heads, key_heads, preferred_element_type=jnp.float32
    ) * (1.0 / math.sqrt(HD))
    return jnp.where(allowed[None], raw_scores, -1000000000.0)


def forward_layer(inputs, allowed, weights):
    gains, shifts, qkv_weight, qv_bias, out_weight, out_bias, up_weight, up_bias, down_weight = (
        weights
    )
    row_count = inputs.shape[0]
    normed_one = layer_norm(inputs, gains[0], shifts[0]).astype(jnp.bfloat16)
    projected = jnp.einsum(
        "rd,dcn->rcn", normed_one, qkv_weight, preferred_element_type=jnp.float32
    )
    queries = (projected[:, 0] + qv_bias[0]).astype(jnp.bfloat16)
    key_rows = projected[:, 1].astype(jnp.bfloat16)
    value_rows = (projected[:, 2] + qv_bias[1]).astype(jnp.bfloat16)
    scores = score_block(queries, key_rows, allowed)
    top = jnp.max(scores, -1, keepdims=True)
    expo = jnp.exp(scores - top)
    total = jnp.sum(expo, -1, keepdims=True)
    probability = expo / total
    logsum = top + jnp.log(total)
    value_heads = value_rows.reshape(row_count, -1, HD)
    attended = jnp.einsum(
        "hqk,khe->qhe",
        probability.astype(jnp.bfloat16),
        value_heads,
        preferred_element_type=jnp.float32,
    )
    attended = attended.reshape(row_count, -1).astype(jnp.bfloat16)
    branch_one = lax.psum(
        jnp.dot(attended, out_weight, preferred_element_type=jnp.float32).astype(jnp.bfloat16),
        "tensor",
    ).astype(jnp.float32)
    middle = inputs + branch_one + out_bias[0]
    normed_two = layer_norm(middle, gains[1], shifts[1]).astype(jnp.bfloat16)
    hidden = jnp.dot(normed_two, up_weight, preferred_element_type=jnp.float32) + up_bias
    activated = jax.nn.gelu(hidden, approximate=True).astype(jnp.bfloat16)
    branch_two = lax.psum(
        jnp.dot(activated, down_weight, preferred_element_type=jnp.float32).astype(jnp.bfloat16),
        "tensor",
    ).astype(jnp.float32)
    saved = (
        inputs,
        middle,
        normed_one,
        queries,
        key_rows,
        value_rows,
        logsum,
        attended,
        normed_two,
        hidden,
        activated,
    )
    return (middle + branch_two + out_bias[1], saved)


def backward_feedforward(grad_out, saved, weights):
    gains, shifts, qkv_weight, qv_bias, out_weight, out_bias, up_weight, up_bias, down_weight = (
        weights
    )
    (
        inputs,
        middle,
        normed_one,
        queries,
        key_rows,
        value_rows,
        logsum,
        attended,
        normed_two,
        hidden,
        activated,
    ) = saved
    grad_low = grad_out.astype(jnp.bfloat16)
    down_grad = jnp.einsum("rf,rd->fd", activated, grad_low, preferred_element_type=jnp.float32)
    grad_active = jnp.einsum("rd,fd->rf", grad_low, down_weight, preferred_element_type=jnp.float32)
    _, gelu_back = jax.vjp(partial(jax.nn.gelu, approximate=True), hidden)
    grad_hidden = gelu_back(grad_active)[0].astype(jnp.bfloat16)
    up_bias_grad = jnp.sum(grad_hidden.astype(jnp.float32), 0)
    up_grad = jnp.einsum("rd,rf->df", normed_two, grad_hidden, preferred_element_type=jnp.float32)
    grad_normed = lax.psum(
        jnp.einsum("rf,df->rd", grad_hidden, up_weight, preferred_element_type=jnp.float32).astype(
            jnp.bfloat16
        ),
        "tensor",
    ).astype(jnp.float32)
    _, norm_back = jax.vjp(layer_norm, middle, gains[1], shifts[1])
    grad_middle, gain_grad, shift_grad = norm_back(grad_normed)
    return (
        grad_out + grad_middle,
        (up_grad, up_bias_grad, down_grad, jnp.sum(grad_out, 0), gain_grad, shift_grad),
    )


def backward_attention(grad_middle, saved, allowed, weights):
    gains, shifts, qkv_weight, qv_bias, out_weight, out_bias, up_weight, up_bias, down_weight = (
        weights
    )
    (
        inputs,
        middle,
        normed_one,
        queries,
        key_rows,
        value_rows,
        logsum,
        attended,
        normed_two,
        hidden,
        activated,
    ) = saved
    row_count = inputs.shape[0]
    scale = 1.0 / math.sqrt(HD)
    grad_low = grad_middle.astype(jnp.bfloat16)
    out_grad = jnp.einsum("rn,rd->nd", attended, grad_low, preferred_element_type=jnp.float32)
    grad_attended = jnp.einsum(
        "rd,nd->rn", grad_low, out_weight, preferred_element_type=jnp.float32
    ).astype(jnp.bfloat16)
    probability = jnp.exp(score_block(queries, key_rows, allowed) - logsum)
    grad_heads = grad_attended.reshape(row_count, -1, HD)
    query_heads = queries.reshape(row_count, -1, HD)
    key_heads = key_rows.reshape(row_count, -1, HD)
    value_heads = value_rows.reshape(row_count, -1, HD)
    grad_prob = jnp.einsum(
        "qhe,khe->hqk", grad_heads, value_heads, preferred_element_type=jnp.float32
    )
    grad_value = jnp.einsum(
        "hqk,qhe->khe",
        probability.astype(jnp.bfloat16),
        grad_heads,
        preferred_element_type=jnp.float32,
    )
    grad_value = grad_value.reshape(row_count, -1).astype(jnp.bfloat16)
    grad_scores = probability * (grad_prob - jnp.sum(grad_prob * probability, -1, keepdims=True))
    grad_scores = grad_scores.astype(jnp.bfloat16)
    grad_query = (
        jnp.einsum("hqk,khe->qhe", grad_scores, key_heads, preferred_element_type=jnp.float32)
        * scale
    )
    grad_query = grad_query.reshape(row_count, -1).astype(jnp.bfloat16)
    grad_key = (
        jnp.einsum("hqk,qhe->khe", grad_scores, query_heads, preferred_element_type=jnp.float32)
        * scale
    )
    grad_key = grad_key.reshape(row_count, -1).astype(jnp.bfloat16)
    grad_project = jnp.stack([grad_query, grad_key, grad_value], 1)
    qkv_grad = jnp.einsum(
        "rd,rcn->dcn", normed_one, grad_project, preferred_element_type=jnp.float32
    )
    qv_bias_grad = jnp.stack(
        [jnp.sum(grad_query.astype(jnp.float32), 0), jnp.sum(grad_value.astype(jnp.float32), 0)]
    )
    grad_normed = lax.psum(
        jnp.einsum(
            "rcn,dcn->rd", grad_project, qkv_weight, preferred_element_type=jnp.float32
        ).astype(jnp.bfloat16),
        "tensor",
    ).astype(jnp.float32)
    _, norm_back = jax.vjp(layer_norm, inputs, gains[0], shifts[0])
    grad_inputs, gain_grad, shift_grad = norm_back(grad_normed)
    return (
        grad_middle + grad_inputs,
        (qkv_grad, qv_bias_grad, out_grad, jnp.sum(grad_middle, 0), gain_grad, shift_grad),
    )


def local(
    tokens,
    cotangent,
    doc_lengths,
    live_mask,
    norm_gains,
    norm_biases,
    query_key_value,
    query_value_bias,
    output_weight,
    output_biases,
    expand_weight,
    expand_bias,
    reduce_weight,
):
    micro_count = tokens.shape[0]
    weights = tuple(
        (
            array[0]
            for array in (
                norm_gains,
                norm_biases,
                query_key_value,
                query_value_bias,
                output_weight,
                output_biases,
                expand_weight,
                expand_bias,
                reduce_weight,
            )
        )
    )
    is_first = lax.axis_index("pipe") == 0
    allowed_list = [
        attention_mask(doc_lengths[index, 0], live_mask[index]) for index in range(micro_count)
    ]
    received = jnp.zeros(tokens.shape[1:], jnp.float32)
    section_outputs = []
    kept_list = []
    for step_index in range(micro_count + 1):
        leading = min(step_index, micro_count - 1)
        trailing = max(step_index - 1, 0)
        section_input = jnp.where(is_first, tokens[leading], received)
        allowed = jnp.where(is_first, allowed_list[leading], allowed_list[trailing])
        layer_out, saved = forward_layer(section_input, allowed, weights)
        section_outputs.append(layer_out)
        kept_list.append(saved)
        if step_index < micro_count:
            received = from_behind(layer_out.astype(jnp.bfloat16), "pipe", 1).astype(
                layer_out.dtype
            )
    activations = jnp.stack(
        [
            jnp.where(is_first, section_outputs[index], section_outputs[index + 1])
            for index in range(micro_count)
        ]
    )[None]
    received = jnp.zeros(tokens.shape[1:], jnp.float32)
    grad_inputs = []
    ff_accum = None
    at_accum = None
    for step_index in range(micro_count + 1):
        early = max(step_index - 1, 0)
        late = min(step_index, micro_count - 1)
        saved = jax.tree.map(
            lambda early_leaf, late_leaf: jnp.where(is_first, early_leaf, late_leaf),
            kept_list[early],
            kept_list[min(step_index + 1, micro_count)],
        )
        allowed = jnp.where(is_first, allowed_list[early], allowed_list[late])
        output_cotangent = cotangent[late] * live_mask[late][:, None].astype(jnp.float32)
        active = jnp.where(
            is_first, 1.0 if step_index >= 1 else 0.0, 1.0 if step_index < micro_count else 0.0
        )
        grad_out = jnp.where(is_first, received, output_cotangent) * active
        grad_middle, ff_terms = backward_feedforward(grad_out, saved, weights)
        ff_accum = ff_terms if ff_accum is None else jax.tree.map(jnp.add, ff_accum, ff_terms)
        grad_input, at_terms = backward_attention(grad_middle, saved, allowed, weights)
        at_accum = at_terms if at_accum is None else jax.tree.map(jnp.add, at_accum, at_terms)
        grad_inputs.append(grad_input)
        if step_index < micro_count:
            received = from_behind(grad_input.astype(jnp.bfloat16), "pipe", -1).astype(
                grad_input.dtype
            )
    up_grad, up_bias_grad, down_grad, down_bias_grad, gain_two, shift_two = ff_accum
    qkv_grad, qv_bias_grad, out_grad, out_bias_grad, gain_one, shift_one = at_accum
    (
        up_grad,
        up_bias_grad,
        down_grad,
        down_bias_grad,
        gain_two,
        shift_two,
        qkv_grad,
        qv_bias_grad,
        out_grad,
        out_bias_grad,
        gain_one,
        shift_one,
    ) = (
        lax.psum(up_grad.astype(jnp.bfloat16), "dp").astype(jnp.float32),
        lax.psum(up_bias_grad.astype(jnp.bfloat16), "dp").astype(jnp.float32),
        lax.psum(down_grad.astype(jnp.bfloat16), "dp").astype(jnp.float32),
        lax.psum(down_bias_grad.astype(jnp.bfloat16), "dp").astype(jnp.float32),
        lax.psum(gain_two.astype(jnp.bfloat16), "dp").astype(jnp.float32),
        lax.psum(shift_two.astype(jnp.bfloat16), "dp").astype(jnp.float32),
        lax.psum(qkv_grad.astype(jnp.bfloat16), "dp").astype(jnp.float32),
        lax.psum(qv_bias_grad.astype(jnp.bfloat16), "dp").astype(jnp.float32),
        lax.psum(out_grad.astype(jnp.bfloat16), "dp").astype(jnp.float32),
        lax.psum(out_bias_grad.astype(jnp.bfloat16), "dp").astype(jnp.float32),
        lax.psum(gain_one.astype(jnp.bfloat16), "dp").astype(jnp.float32),
        lax.psum(shift_one.astype(jnp.bfloat16), "dp").astype(jnp.float32),
    )
    input_grads = jnp.stack(
        [
            jnp.where(is_first, grad_inputs[index + 1], grad_inputs[index])
            for index in range(micro_count)
        ]
    )[None]
    return (
        activations,
        input_grads,
        jnp.stack([gain_one, gain_two])[None],
        jnp.stack([shift_one, shift_two])[None],
        qkv_grad[None],
        qv_bias_grad[None],
        out_grad[None],
        jnp.stack([out_bias_grad, down_bias_grad])[None],
        up_grad[None],
        up_bias_grad[None],
        down_grad[None],
    )


def solution(mesh):
    in_specs = (
        P(None, "dp", None),
        P(None, "dp", None),
        P(None, "dp", None),
        P(None, "dp"),
        P("pipe", None, None),
        P("pipe", None, None),
        P("pipe", None, None, "tensor"),
        P("pipe", None, "tensor"),
        P("pipe", "tensor", None),
        P("pipe", None, None),
        P("pipe", None, "tensor"),
        P("pipe", "tensor"),
        P("pipe", "tensor", None),
    )
    out_specs = (
        P("pipe", None, "dp", None),
        P("pipe", None, "dp", None),
        P("pipe", None, None),
        P("pipe", None, None),
        P("pipe", None, None, "tensor"),
        P("pipe", None, "tensor"),
        P("pipe", "tensor", None),
        P("pipe", None, None),
        P("pipe", None, "tensor"),
        P("pipe", "tensor"),
        P("pipe", "tensor", None),
    )
    return jax.shard_map(local, mesh=mesh, in_specs=in_specs, out_specs=out_specs, check_vma=False)
```

profile of v0, /device:TPU:1, one launch (start us, length us, event | category | flops | bytes accessed | tf_op | source)
XLA Modules:
  0.0 890.3 jit_solution(7145154293292134148)
XLA Ops:
  17.3 42.8 %all-reduce.20.cloned.1.call-done = bf16[80,1024]{1,0:T(8,128)(2,1)} async-done(((bf16[80,1024]{1,0:T(8,128)(2,1)}), bf16[80,1024]{1,0:T(8,128)(2,1)}) %all-reduce.20.cloned.1.call-update) | async-done | bytes 163856 | tf_op jit(solution)/shard_map/psum | solution.py:71
  65.7 42.0 %all-reduce.22.cloned.1.call-done = bf16[80,1024]{1,0:T(8,128)(2,1)} async-done(((bf16[80,1024]{1,0:T(8,128)(2,1)}), bf16[80,1024]{1,0:T(8,128)(2,1)}) %all-reduce.22.cloned.1.call-update) | async-done | bytes 163856 | tf_op jit(solution)/shard_map/psum | solution.py:79
  108.6 4.6 collective-permute-start
  130.5 42.4 %all-reduce.24.cloned.1.call-done = bf16[80,1024]{1,0:T(8,128)(2,1)} async-done(((bf16[80,1024]{1,0:T(8,128)(2,1)}), bf16[80,1024]{1,0:T(8,128)(2,1)}) %all-reduce.24.cloned.1.call-update) | async-done | bytes 163856 | tf_op jit(solution)/shard_map/psum | solution.py:71
  184.5 3.8 fusion.282
  188.2 38.9 %all-reduce.42.cloned.1.call-done = (bf16[80,1024]{1,0:T(8,128)(2,1)}, bf16[80,1024]{1,0:T(8,128)(2,1)}) async-done(((bf16[80,1024]{1,0:T(8,128)(2,1)}, bf16[80,1024]{1,0:T(8,128)(2,1)}), (bf16[80,1024]{1,0:T(8,128)(2,1)}, bf16[80,1024]{1,0:T(8,128)(2,1)})) %all-reduce.42.cloned.1.call-update) | async-done | bytes 327696 | tf_op jit(solution)/shard_map/psum | solution.py:79
  244.1 3.8 collective-permute-start.1
  265.1 3.5 fusion.263
  269.2 40.0 %all-reduce.40.cloned.1.call-done = (bf16[80,1024]{1,0:T(8,128)(2,1)}, bf16[80,1024]{1,0:T(8,128)(2,1)}) async-done(((bf16[80,1024]{1,0:T(8,128)(2,1)}, bf16[80,1024]{1,0:T(8,128)(2,1)}), (bf16[80,1024]{1,0:T(8,128)(2,1)}, bf16[80,1024]{1,0:T(8,128)(2,1)})) %all-reduce.40.cloned.1.call-update) | async-done | bytes 327696 | tf_op jit(solution)/shard_map/psum | solution.py:71
  328.5 4.0 fusion.274
  335.4 37.7 %all-reduce.38.cloned.1.call-done = (bf16[80,1024]{1,0:T(8,128)(2,1)}, bf16[80,1024]{1,0:T(8,128)(2,1)}) async-done(((bf16[80,1024]{1,0:T(8,128)(2,1)}, bf16[80,1024]{1,0:T(8,128)(2,1)}), (bf16[80,1024]{1,0:T(8,128)(2,1)}, bf16[80,1024]{1,0:T(8,128)(2,1)})) %all-reduce.38.cloned.1.call-update) | async-done | bytes 327696 | tf_op jit(solution)/shard_map/psum | solution.py:79
  379.0 5.4 collective-permute-start.2
  428.6 3.5 fusion.261
  432.2 37.0 %all-reduce.36.cloned.1.call-done = (bf16[80,1024]{1,0:T(8,128)(2,1)}, bf16[80,1024]{1,0:T(8,128)(2,1)}) async-done(((bf16[80,1024]{1,0:T(8,128)(2,1)}, bf16[80,1024]{1,0:T(8,128)(2,1)}), (bf16[80,1024]{1,0:T(8,128)(2,1)}, bf16[80,1024]{1,0:T(8,128)(2,1)})) %all-reduce.36.cloned.1.call-update) | async-done | bytes 327696 | tf_op jit(solution)/shard_map/psum | solution.py:71
  490.3 4.0 fusion.272
  497.2 36.2 %all-reduce.26.cloned.1.call-done = bf16[80,1024]{1,0:T(8,128)(2,1)} async-done(((bf16[80,1024]{1,0:T(8,128)(2,1)}), bf16[80,1024]{1,0:T(8,128)(2,1)}) %all-reduce.26.cloned.1.call-update) | async-done | bytes 163856 | tf_op jit(solution)/shard_map/psum | solution.py:123
  557.2 39.6 %all-reduce.28.cloned.1.call-done = bf16[80,1024]{1,0:T(8,128)(2,1)} async-done(((bf16[80,1024]{1,0:T(8,128)(2,1)}), bf16[80,1024]{1,0:T(8,128)(2,1)}) %all-reduce.28.cloned.1.call-update) | async-done | bytes 163856 | tf_op jit(solution)/shard_map/psum | solution.py:195
  604.3 5.0 collective-permute-done.5
  614.1 7.3 fusion
  625.5 30.1 %all-reduce.30.cloned.1.call-done = bf16[80,1024]{1,0:T(8,128)(2,1)} async-done(((bf16[80,1024]{1,0:T(8,128)(2,1)}), bf16[80,1024]{1,0:T(8,128)(2,1)}) %all-reduce.30.cloned.1.call-update) | async-done | bytes 163856 | tf_op jit(solution)/shard_map/psum | solution.py:123
  670.2 5.6 fusion.50
  681.5 29.8 %all-reduce.34.cloned.1.call-done = (bf16[80,1024]{1,0:T(8,128)(2,1)}, bf16[80,1024]{1,0:T(8,128)(2,1)}) async-done(((bf16[80,1024]{1,0:T(8,128)(2,1)}, bf16[80,1024]{1,0:T(8,128)(2,1)}), (bf16[80,1024]{1,0:T(8,128)(2,1)}, bf16[80,1024]{1,0:T(8,128)(2,1)})) %all-reduce.34.cloned.1.call-update) | async-done | bytes 327696 | tf_op jit(solution)/shard_map/psum | solution.py:79
  713.8 53.0 %all-reduce = (bf16[1,1024]{1,0:T(2,128)(2,1)S(1)}, bf16[1,1024]{1,0:T(2,128)(2,1)S(1)}, bf16[1,1024]{1,0:T(2,128)(2,1)S(1)}, bf16[1,1024]{1,0:T(2,128)(2,1)S(1)...) all-reduce(bf16[1,1024]{1,0:T(2,128)(2,1)S(1)} %stack.133, ...), channel_id=1, replica_groups=mesh['pipe'=2,'dp'=16,'tensor'=4] {'dp'}, use_global_device_ids=true, to_apply=%region_91.92 | all-reduce | flops 7680 | bytes 30720 | tf_op jit(solution)/shard_map/psum | solution.py:313
  775.3 98.0 %all-reduce.32.cloned.1.call-done = (bf16[1,1024,3,256]{3,1,2,0:T(8,128)(2,1)}, bf16[1,256,1024]{2,1,0:T(8,128)(2,1)}, bf16[1,1024,1024]{2,1,0:T(8,128)(2,1)}, bf16[1,1024,1024]{2,1,0:T(8,128)(2,1)}) async-done(((bf16[1,1024,3,256]{3,1,2,0:T(8,128)(2,1)}, bf16[1,256,1024]{2,1,0:T(8,128)(2,1)}, bf16[1,1024,1024]{2,1,0:T(8,128)(2,1)}, bf16[1,1024,1024]{2,1,0:T(8,128)(2,1)}), ...) | async-done | bytes 6291472 | tf_op jit(solution)/shard_map/psum | solution.py:315
  (717 shorter events, 254.5 us)
Async XLA Ops:
  7.2 52.8 %all-reduce.20.cloned.1.call-start = ((), (), s32[]{:S(2)}) async-start(), calls=%async_computation | async-start | bytes 327680 | tf_op jit(solution)/shard_map/psum | solution.py:71
  11.3 173.1 %copy-start.96 = (f32[1,1,1024]{2,1,0:T(1,128)}, f32[1,1,1024]{2,1,0:T(1,128)S(1)}, u32[]{:S(2)}) copy-start(f32[1,1,1024]{2,1,0:T(1,128)S(1)} %get-tuple-element.134) | copy-start | bytes 12292
  14.3 108.9 %copy-start.119 = (f32[4,64]{1,0:T(4,128)}, f32[4,64]{1,0:T(4,128)S(1)}, u32[]{:S(2)}) copy-start(f32[4,64]{1,0:T(4,128)S(1)} %add.684) | copy-start | bytes 3076
  14.4 110.6 %copy-start.116 = (f32[4,64]{1,0:T(4,128)}, f32[4,64]{1,0:T(4,128)S(1)}, u32[]{:S(2)}) copy-start(f32[4,64]{1,0:T(4,128)S(1)} %add.681) | copy-start | bytes 3076
  16.0 110.4 %copy-start.125 = (f32[4,80]{1,0:T(4,128)}, f32[4,80]{1,0:T(4,128)S(1)}, u32[]{:S(2)}) copy-start(f32[4,80]{1,0:T(4,128)S(1)} %get-tuple-element.172) | copy-start | bytes 3844
  16.1 110.3 %copy-start.132 = (f32[4,80]{1,0:T(4,128)}, f32[4,80]{1,0:T(4,128)S(1)}, u32[]{:S(2)}) copy-start(f32[4,80]{1,0:T(4,128)S(1)} %fusion.311) | copy-start | bytes 3844
  17.2 90.5 %all-reduce.22.cloned.1.call-start = ((), (), s32[]{:S(2)}) async-start(), calls=%async_computation.1 | async-start | bytes 327680 | tf_op jit(solution)/shard_map/psum | solution.py:79
  17.3 155.7 %copy-start.108 = (f32[1,1,1024]{2,1,0:T(1,128)}, f32[1,1,1024]{2,1,0:T(1,128)S(1)}, u32[]{:S(2)}) copy-start(f32[1,1,1024]{2,1,0:T(1,128)S(1)} %get-tuple-element.137) | copy-start | bytes 12292
  65.6 107.3 %all-reduce.24.cloned.1.call-start = ((), (), s32[]{:S(2)}) async-start(), calls=%async_computation.2 | async-start | bytes 327680 | tf_op jit(solution)/shard_map/psum | solution.py:71
  108.6 6.9 collective-permute-start
  129.1 98.1 %all-reduce.42.cloned.1.call-start = ((), (), s32[]{:S(2)}) async-start(), calls=%async_computation.11 | async-start | bytes 655360 | tf_op jit(solution)/shard_map/psum | solution.py:79
  184.4 124.8 %all-reduce.40.cloned.1.call-start = ((), (), s32[]{:S(2)}) async-start(), calls=%async_computation.10 | async-start | bytes 655360 | tf_op jit(solution)/shard_map/psum | solution.py:71
  244.1 6.5 collective-permute-start.1
  264.9 108.2 %all-reduce.38.cloned.1.call-start = ((), (), s32[]{:S(2)}) async-start(), calls=%async_computation.9 | async-start | bytes 655360 | tf_op jit(solution)/shard_map/psum | solution.py:79
  314.8 8.9 collective-permute-start.3
  328.5 140.7 %all-reduce.36.cloned.1.call-start = ((), (), s32[]{:S(2)}) async-start(), calls=%async_computation.8 | async-start | bytes 655360 | tf_op jit(solution)/shard_map/psum | solution.py:71
  379.0 9.0 %collective-permute-start.2 = (bf16[80,1024]{1,0:T(8,128)(2,1)}, bf16[80,1024]{1,0:T(8,128)(2,1)}, u32[]{:S(2)}, u32[]{:S(2)}) collective-permute-start(bf16[80,1024]{1,0:T(8,128)(2,1)} %get-tuple-element.117), channel_id=1, source_target_pairs={{0,64},{1,65},{2,66},{3,67},{4,68},{5,69},{6,70},{7,71},{8,72},{9,... | collective-permute-start | bytes 491528 | tf_op jit(solution)/shard_map/ppermute | solution.py:15
  425.4 108.0 %all-reduce.26.cloned.1.call-start = ((), (), s32[]{:S(2)}) async-start(), calls=%async_computation.3 | async-start | bytes 327680 | tf_op jit(solution)/shard_map/psum | solution.py:123
  478.0 7.6 collective-permute-start.4
  490.2 106.7 %all-reduce.28.cloned.1.call-start = ((), (), s32[]{:S(2)}) async-start(), calls=%async_computation.4 | async-start | bytes 327680 | tf_op jit(solution)/shard_map/psum | solution.py:195
  554.0 101.6 %all-reduce.30.cloned.1.call-start = ((), (), s32[]{:S(2)}) async-start(), calls=%async_computation.5 | async-start | bytes 327680 | tf_op jit(solution)/shard_map/psum | solution.py:123
  601.7 7.6 collective-permute-start.5
  613.9 97.3 %all-reduce.34.cloned.1.call-start = ((), (), s32[]{:S(2)}) async-start(), calls=%async_computation.7 | async-start | bytes 655360 | tf_op jit(solution)/shard_map/psum | solution.py:79
  667.5 205.8 %all-reduce.32.cloned.1.call-start = ((), (), s32[]{:S(2)}) async-start(), calls=%async_computation.6 | async-start | bytes 12582912 | tf_op jit(solution)/shard_map/psum | solution.py:315
  (202 other events, 2302.0 us)
Sparse Core Ops, SparseCore 0:
  17.3 42.7 all-reduce.19
  65.7 41.8 all-reduce.21
  129.2 43.6 all-reduce.23
  184.5 42.6 all-reduce.41
  265.0 44.1 all-reduce.39
  328.6 44.5 all-reduce.37
  425.5 43.5 all-reduce.35
  490.3 43.0 all-reduce.25
  554.1 42.7 all-reduce.27
  614.0 41.5 all-reduce.29
  667.6 43.5 all-reduce.33
  714.5 158.8 all-reduce.31
where the time goes:
time: 902 us; the launch traced here: 890 us
  waiting for transfers between devices  522 us (58%)
  matrix products  136 us (15%)
  other arithmetic  103 us (11%)
  blocking collectives  53 us (6%)
  local copies, waits for them, and re-layouts  39.2 us (4%)
  starting transfers between devices  18.9 us (2%)
  between operations  17.5 us (2%)
    psum x4, waiting for transfers between devices, forward_layer(): lax.psum(jnp.dot(attended, out_weight, preferred_element_type=jnp.float32...  162 us
    psum x4, waiting for transfers between devices, forward_layer(): lax.psum(jnp.dot(activated, down_weight, preferred_element_type=jnp.float...  148 us
    psum x1, waiting for transfers between devices, local(): lax.psum(qkv_grad.astype(jnp.bfloat16), 'dp').astype(jnp.float32)  98 us
    psum x2, waiting for transfers between devices, backward_feedforward(): lax.psum(jnp.einsum('rf,df->rd', grad_hidden, up_weight, preferred_elemen...  66.3 us
    psum x1, blocking collectives, local(): lax.psum(gain_two.astype(jnp.bfloat16), 'dp').astype(jnp.float32)  53 us
    psum x1, waiting for transfers between devices, backward_attention(): lax.psum(jnp.einsum('rcn,dcn->rd', grad_project, qkv_weight, preferred_el...  39.6 us
    reduce_sum x16, other arithmetic, layer_norm(): center = inputs - jnp.mean(inputs, -1, keepdims=True)  22.4 us
    dot_general x4, matrix products, backward_feedforward(): jnp.einsum('rf,rd->fd', activated, grad_low, preferred_element_type=jnp.f...  18.2 us
  transfers between devices with their start and end apart: 18, of which 15 were waited for; matrix products, arithmetic and copies ran while one was open for 10% of the time, Pallas kernels for 0%

commit v1 on v0

v1 whole, which is shorter than its diff:
```python
import functools
import math

import jax
import jax.numpy as jnp
from jax import lax
from jax.experimental import pallas as pl
from jax.experimental.pallas import tpu as pltpu
from jax.sharding import PartitionSpec as P

MESH = pl.DeviceIdType.MESH
F32 = jnp.float32
BF16 = jnp.bfloat16
D = 1024
ROWS = 80
SLOTS = 3
USED = ROWS * SLOTS
PAD = 256
TEN = 4
CH = PAD // TEN
HEADS = 4
HD = 64
W = 256
BUCKETS = ((1024, 1024, 256, 256), (1024, 1024, 256, 256), (256, 1024, 128, 0), (1024, 768, 256, 256))
A1, Y1, A2, Y2, OUT, DOUT, DA2, DY1, DA1, DX, SMALL = range(11)


def dot_nn(a, b):
    return lax.dot_general(a, b, (((1,), (0,)), ((), ())), preferred_element_type=F32)


def dot_nt(a, b):
    return lax.dot_general(a, b, (((1,), (1,)), ((), ())), preferred_element_type=F32)


def dot_tn(a, b):
    return lax.dot_general(a, b, (((0,), (0,)), ((), ())), preferred_element_type=F32)


def tile(j, size=W):
    return pl.ds(pl.multiple_of(j * size, size), size)


def normed(u):
    center = u - jnp.mean(u, -1, keepdims=True)
    inverse = lax.rsqrt(jnp.mean(center * center, -1, keepdims=True) + 1e-05)
    return center * inverse, inverse


def norm_back(grad, u, gain):
    unit, inverse = normed(u)
    scaled = grad * gain
    along = jnp.mean(scaled * unit, -1, keepdims=True)
    grad_u = inverse * (scaled - jnp.mean(scaled, -1, keepdims=True) - unit * along)
    return grad_u, jnp.sum(grad * unit, 0, keepdims=True), jnp.sum(grad, 0, keepdims=True)


def kernel(
    reduce_dp,
    tok_hbm, cot_hbm, docs, live, gains, shifts, wqkv_hbm, qvb, wo_hbm, obias, wup_hbm, upb, wdn_hbm,
    act_out, dx_out, gdn_out, gup_out, go_out, gqkv_out, small_out,
    tok, cot, wqkv, wo, wup, wdn, mask, xc, a1, qkv, prob, att, y1s, y1r, x2c, a2, slope, g,
    y2s, y2r, actg, doc, dy2, dg, dh, da2s, da2r, dx2c, dy1, dqkv, da1s, da1r, dxg,
    pipe_f, pipe_b, pipe_fs, pipe_bs, sm, smz, smc, smy, smx, acc0, acc1, acc2,
    wg0, wg1, wg2, wg3, rc0, rc1, rc2, rc3, p10, p11, p12, p13, q10, q11, q13,
    p20, p21, p22, p23, q20, q21, q23,
    load_sem, out_sem, tp_s, tp_r, pp_s, pp_r, dp_s, dp_r, dp_l, sd_s, sd_r,
):
    wgs, rcs = (wg0, wg1, wg2, wg3), (rc0, rc1, rc2, rc3)
    p1s, q1s = (p10, p11, p12, p13), (q10, q11, None, q13)
    p2s, q2s = (p20, p21, p22, p23), (q20, q21, None, q23)
    gouts = (gdn_out, gup_out, go_out, gqkv_out)
    pipe = lax.axis_index("pipe")
    dp = lax.axis_index("dp")
    z = lax.axis_index("tensor")
    first = pipe == 0
    second = pipe == 1
    gx, gy, gc = dp // 4, (dp // 2) % 2, dp % 2
    core_peer = gx * 4 + gy * 2 + (1 - gc)
    y_peer = gx * 4 + (1 - gy) * 2 + gc
    x_peers = [((gx + t) % 4) * 4 + gy * 2 + gc for t in (1, 2, 3)]
    mine = tile(z, CH)

    def load(k, src, dst):
        return pltpu.make_async_copy(src, dst, load_sem.at[k])

    loads = {
        "tok": load(0, tok_hbm, tok.at[pl.ds(0, USED)]),
        "cot": load(1, cot_hbm, cot.at[pl.ds(0, USED)]),
        "qkv": load(2, wqkv_hbm, wqkv),
        "o": load(3, wo_hbm, wo),
        "up": load(4, wup_hbm, wup),
        "dn": load(5, wdn_hbm, wdn),
    }
    for name in ("tok", "cot", "qkv", "o", "up", "dn"):
        loads[name].start()

    barrier = pltpu.get_barrier_semaphore()
    partners = [{"tensor": (z + t) % 4} for t in (1, 2, 3)] + [{"pipe": 1 - pipe}]
    if reduce_dp:
        partners += [{"dp": core_peer}, {"dp": y_peer}] + [{"dp": p} for p in x_peers]
    for partner in partners:
        pl.semaphore_signal(barrier, inc=1, device_id=partner, device_id_type=MESH)

    def places(shape, axis):
        at = lax.broadcasted_iota(jnp.int32, shape, axis)
        slot = (at >= ROWS).astype(jnp.int32) + (at >= 2 * ROWS).astype(jnp.int32)
        slot = slot + (at >= 3 * ROWS).astype(jnp.int32)
        spot = at - ROWS * slot
        segment = 4 * slot
        alive = jnp.zeros(shape, F32)
        for s in range(SLOTS):
            end = jnp.int32(0)
            for k in range(3):
                end = end + docs[s, k]
                segment = segment + jnp.where((slot == s) & (spot >= end), 1, 0)
            alive = jnp.where((slot == s) & (spot.astype(F32) < counts[s : s + 1, :]), 1.0, alive)
        return at, segment, alive

    counts = jnp.sum(live[...].astype(F32), 1, keepdims=True)
    row_at, row_segment, row_live = places((PAD, 1), 0)
    col_at, col_segment, col_live = places((1, PAD), 1)
    seen = (row_segment == col_segment) & (col_at <= row_at)
    seen = seen & ((col_live + jnp.where(row_at == col_at, 1.0, 0.0)) > 0.5)
    mask[...] = jnp.where(seen, 1.0, 0.0)
    sm[...] = jnp.zeros_like(sm)
    head_of = lax.broadcasted_iota(jnp.int32, (1, W), 1) // HD

    pl.semaphore_wait(barrier, len(partners))

    def tp_copy(k, t, src, dst):
        return pltpu.make_async_remote_copy(
            src_ref=src,
            dst_ref=dst,
            send_sem=tp_s.at[k, t - 1],
            recv_sem=tp_r.at[k, t - 1],
            device_id={"tensor": (z + t) % 4},
            device_id_type=MESH,
        )

    def scatter(k, src, dst):
        return [tp_copy(k, t, src.at[tile((z + t) % 4, CH)], dst.at[t - 1]) for t in (2, 1, 3)]

    def gather(k, buf):
        return [tp_copy(k, t, buf.at[mine], buf.at[mine]) for t in (2, 1, 3)]

    def start(copies):
        for copy in copies:
            copy.start()

    def arrive(copies):
        for copy in copies:
            copy.wait_recv()

    def sent(copies):
        for copy in copies:
            copy.wait_send()

    ex = {
        A1: gather(A1, a1),
        Y1: scatter(Y1, y1s, y1r),
        A2: gather(A2, a2),
        Y2: scatter(Y2, y2s, y2r),
        OUT: gather(OUT, actg),
        DOUT: gather(DOUT, dy2),
        DA2: scatter(DA2, da2s, da2r),
        DY1: gather(DY1, dy1),
        DA1: scatter(DA1, da1s, da1r),
        DX: gather(DX, dxg),
        SMALL: [tp_copy(SMALL, t, smz.at[z], smz.at[z]) for t in (2, 1, 3)],
    }
    forth = pltpu.make_async_remote_copy(
        src_ref=pipe_fs, dst_ref=pipe_f, send_sem=pp_s.at[0], recv_sem=pp_r.at[0],
        device_id={"pipe": 1 - pipe}, device_id_type=MESH,
    )
    back = pltpu.make_async_remote_copy(
        src_ref=pipe_bs, dst_ref=pipe_b, send_sem=pp_s.at[1], recv_sem=pp_r.at[1],
        device_id={"pipe": 1 - pipe}, device_id_type=MESH,
    )

    def summed(src, dst):
        total = src[mine].astype(F32)
        for t in range(3):
            total = total + dst[t].astype(F32)
        return total

    def dp_copy(b, k, src, dst, peer):
        return pltpu.make_async_remote_copy(
            src_ref=src, dst_ref=dst, send_sem=dp_s.at[b, k], recv_sem=dp_r.at[b, k],
            device_id={"dp": peer}, device_id_type=MESH,
        )

    def rows(at, size):
        return pl.ds(pl.multiple_of(at, 16), size)

    def add_into(dst, at, size, terms):
        step = min(size, 64)

        @pl.loop(0, size // step)
        def _(i):
            off = pl.multiple_of(i * step, 16)
            total = dst[rows(at + off, step), :].astype(F32)
            for term in terms:
                total = total + term(off, step).astype(F32)
            dst[rows(at + off, step), :] = total.astype(BF16)

    def bucket(b):
        size, _, p, q = BUCKETS[b]
        half = size // 2
        wg, rc, out = wgs[b], rcs[b], gouts[b]
        p1, q1, p2, q2 = p1s[b], q1s[b], p2s[b], q2s[b]
        base = gc * half
        p8, p4, q8, q2n = p // 8, p // 4, q // 8, q // 2
        c = {}
        c["core"] = [dp_copy(b, 0, wg.at[rows((1 - gc) * half, half)], rc, core_peer)]
        xs = [(gx + t) % 4 for t in (1, 2, 3)]
        order = (1, 0, 2)
        c["p1"] = [
            dp_copy(b, 1 + i, rc.at[rows(xs[i] * p4, p4)], p1.at[i], x_peers[i]) for i in order
        ]
        p_fin = gx * p4 + gy * p8
        c["p2"] = [dp_copy(b, 5, rc.at[rows(gx * p4 + (1 - gy) * p8, p8)], p2, y_peer)]
        c["p3"] = [dp_copy(b, 9, rc.at[rows(p_fin, p8)], out.at[rows(base + p_fin, p8)], y_peer)]
        p_part = out.at[rows(base + gx * p4, p4)]
        c["p4"] = [dp_copy(b, 13 + i, p_part, p_part, x_peers[i]) for i in order]
        half_out = out.at[rows(base, half)]
        c["all"] = [dp_copy(b, 17, half_out, half_out, core_peer)]
        keep = [
            pltpu.make_async_copy(
                rc.at[rows(p_fin, p8)], out.at[rows(base + p_fin, p8)], dp_l.at[b, 0]
            )
        ]
        if q:
            q_fin = p + gy * q2n + gx * q8
            c["q1"] = [dp_copy(b, 4, rc.at[rows(p + (1 - gy) * q2n, q2n)], q1, y_peer)]
            c["q2"] = [
                dp_copy(b, 6 + i, rc.at[rows(p + gy * q2n + xs[i] * q8, q8)], q2.at[i], x_peers[i])
                for i in order
            ]
            c["q3"] = [
                dp_copy(b, 10 + i, rc.at[rows(q_fin, q8)], out.at[rows(base + q_fin, q8)], x_peers[i])
                for i in order
            ]
            q_part = out.at[rows(base + p + gy * q2n, q2n)]
            c["q4"] = [dp_copy(b, 16, q_part, q_part, y_peer)]
            keep.append(
                pltpu.make_async_copy(
                    rc.at[rows(q_fin, q8)], out.at[rows(base + q_fin, q8)], dp_l.at[b, 1]
                )
            )

        def step0():
            start(c["core"])

        def step1():
            arrive(c["core"])
            add_into(rc, 0, half, [lambda o, n: wg[rows(base + o, n), :]])
            start(c["p1"])
            if q:
                start(c["q1"])

        def step2():
            if q:
                arrive(c["q1"])
                add_into(rc, p + gy * q2n, q2n, [lambda o, n: q1[rows(o, n), :]])
                start(c["q2"])
            arrive(c["p1"])
            add_into(rc, gx * p4, p4, [
                (lambda o, n, i=i: p1[i, rows(o, n), :]) for i in range(3)
            ])
            start(c["p2"])

        def step3():
            arrive(c["p2"])
            add_into(rc, p_fin, p8, [lambda o, n: p2[rows(o, n), :]])
            start(c["p3"])
            keep[0].start()
            if q:
                arrive(c["q2"])
                add_into(rc, q_fin, q8, [
                    (lambda o, n, i=i: q2[i, rows(o, n), :]) for i in range(3)
                ])
                start(c["q3"])
                keep[1].start()

        def step4():
            keep[0].wait()
            arrive(c["p3"])
            start(c["p4"])
            if q:
                keep[1].wait()
                arrive(c["q3"])
                start(c["q4"])

        def step5():
            arrive(c["p4"])
            if q:
                arrive(c["q4"])
            start(c["all"])

        def step6():
            arrive(c["all"])
            for group in c.values():
                sent(group)

        return [step0, step1, step2, step3, step4, step5, step6]

    def sd_copy(k, src, dst, peer):
        return pltpu.make_async_remote_copy(
            src_ref=src, dst_ref=dst, send_sem=sd_s.at[k], recv_sem=sd_r.at[k],
            device_id={"dp": peer}, device_id_type=MESH,
        )

    @pl.when(first)
    def _():
        loads["tok"].wait()
        tok[pl.ds(USED, PAD - USED), :] = jnp.zeros((PAD - USED, D), F32)

        @pl.loop(0, TEN)
        def _(i):
            unit, _ = normed(tok[tile(i, CH), :])
            a1[tile(i, CH), :] = (unit * gains[0:1, :] + shifts[0:1, :]).astype(BF16)

        xc[...] = tok[mine, :]
        loads["cot"].wait()
        loads["dn"].wait()

    def output_grads():
        @pl.loop(0, D // W)
        def _(j):
            dg[:, tile(j)] = dot_nt(dy2[...], wdn[tile(j), :])

    @pl.when(second)
    def _():
        loads["cot"].wait()
        cot[pl.ds(USED, PAD - USED), :] = jnp.zeros((PAD - USED, D), F32)
        masked = cot[...] * row_live
        cot[...] = masked
        dy2[...] = masked.astype(BF16)
        sm[5:6, :] = jnp.sum(masked, 0, keepdims=True)
        doc[...] = cot[mine, :]
        loads["dn"].wait()
        output_grads()
        loads["tok"].wait()
        forth.wait_recv()
        inputs = pipe_f[...].astype(F32)
        xc[...] = inputs
        unit, _ = normed(inputs)
        a1[mine, :] = (unit * gains[0:1, :] + shifts[0:1, :]).astype(BF16)
        start(ex[A1])
        arrive(ex[A1])

    loads["qkv"].wait()
    for j in range(3):
        part = dot_nn(a1[...], wqkv[:, j * W : (j + 1) * W])
        if j != 1:
            part = part + qvb[j // 2 : j // 2 + 1, :]
        qkv[:, j * W : (j + 1) * W] = part.astype(BF16)

    def head_rows(values, h):
        return (values.astype(F32) * jnp.where(head_of == h, 1.0, 0.0)).astype(BF16)

    acc0[...] = jnp.zeros_like(acc0)

    @pl.loop(0, HEADS)
    def _(h):
        scores = dot_nt(head_rows(qkv[:, 0:W], h), qkv[:, W : 2 * W]) * (1.0 / math.sqrt(HD))
        scores = jnp.where(mask[...] > 0.5, scores, -1000000000.0)
        expo = jnp.exp(scores - jnp.max(scores, -1, keepdims=True))
        p = expo / jnp.sum(expo, -1, keepdims=True)
        prob[h] = p
        acc0[...] += dot_nn(p.astype(BF16), head_rows(qkv[:, 2 * W : 3 * W], h))

    att[...] = acc0[...].astype(BF16)
    loads["o"].wait()

    @pl.loop(0, D // W)
    def _(j):
        y1s[:, tile(j)] = dot_nn(att[...], wo[:, tile(j)]).astype(BF16)

    start(ex[Y1])
    arrive(ex[Y1])
    middle = xc[...] + summed(y1s, y1r) + obias[0:1, :]
    x2c[...] = middle
    unit, _ = normed(middle)
    a2[mine, :] = (unit * gains[1:2, :] + shifts[1:2, :]).astype(BF16)
    start(ex[A2])
    loads["up"].wait()
    arrive(ex[A2])

    @pl.loop(0, D // W)
    def _(j):
        hidden = dot_nn(a2[...], wup[:, tile(j)]) + upb[:, tile(j)]
        square = hidden * hidden
        root = math.sqrt(2.0 / math.pi)
        bent = jnp.tanh(root * hidden * (1.0 + 0.044715 * square))
        lifted = 0.5 * (1.0 + bent)
        g[:, tile(j)] = (hidden * lifted).astype(BF16)
        inner = root * (1.0 + 3.0 * 0.044715 * square)
        slope[:, tile(j)] = lifted + 0.5 * hidden * (1.0 - bent * bent) * inner

    def down():
        @pl.loop(0, D // W)
        def _(j):
            y2s[:, tile(j)] = dot_nn(g[...], wdn[:, tile(j)]).astype(BF16)

        start(ex[Y2])

    def layer_output():
        arrive(ex[Y2])
        result = (x2c[...] + summed(y2s, y2r) + obias[1:2, :]).astype(BF16)
        pipe_fs[...] = result
        actg[mine, :] = result

    act_copy = pltpu.make_async_copy(actg.at[pl.ds(0, USED)], act_out, out_sem.at[0])

    @pl.when(first)
    def _():
        down()
        layer_output()
        forth.start()
        start(ex[OUT])
        back.wait_recv()
        dy2[mine, :] = pipe_b[...]
        doc[...] = pipe_b[...].astype(F32)
        start(ex[DOUT])
        arrive(ex[DOUT])
        output_grads()

    @pl.loop(0, D // W)
    def _(j):
        grad = (dg[:, tile(j)] * slope[:, tile(j)]).astype(BF16)
        dh[:, tile(j)] = grad
        sm[7:8, tile(j)] = jnp.sum(grad.astype(F32), 0, keepdims=True)

    @pl.loop(0, D // W)
    def _(j):
        da2s[:, tile(j)] = dot_nt(dh[...], wup[tile(j), :]).astype(BF16)

    start(ex[DA2])

    @pl.when(first)
    def _():
        sm[5:6, :] = jnp.sum(dy2[...].astype(F32), 0, keepdims=True)

    @pl.loop(0, D // W)
    def _(j):
        wgs[0][tile(j), :] = dot_tn(g[:, tile(j)], dy2[...]).astype(BF16)

    @pl.loop(0, D // W)
    def _(j):
        wgs[1][tile(j), :] = dot_tn(a2[:, tile(j)], dh[...]).astype(BF16)

    arrive(ex[DA2])
    grad_u, gain_grad, shift_grad = norm_back(summed(da2s, da2r), x2c[...], gains[1:2, :])
    grad_middle = doc[...] + grad_u
    dx2c[...] = grad_middle
    sm[1:2, :] = gain_grad
    sm[3:4, :] = shift_grad
    sm[4:5, :] = jnp.sum(grad_middle, 0, keepdims=True)
    dy1[mine, :] = grad_middle.astype(BF16)
    start(ex[DY1])
    arrive(ex[DY1])

    att_grad = dot_nt(dy1[...], wo[...]).astype(BF16)
    dqkv[:, 2 * W : 3 * W] = att_grad
    acc0[...] = jnp.zeros_like(acc0)
    acc1[...] = jnp.zeros_like(acc1)
    acc2[...] = jnp.zeros_like(acc2)

    @pl.loop(0, HEADS)
    def _(h):
        p = prob[h]
        own = head_rows(dqkv[:, 2 * W : 3 * W], h)
        grad_p = dot_nt(own, qkv[:, 2 * W : 3 * W])
        acc2[...] += dot_tn(p.astype(BF16), own)
        grad_s = p * (grad_p - jnp.sum(grad_p * p, -1, keepdims=True))
        grad_s = grad_s.astype(BF16)
        acc0[...] += dot_nn(grad_s, head_rows(qkv[:, W : 2 * W], h))
        acc1[...] += dot_tn(grad_s, head_rows(qkv[:, 0:W], h))

    scale = 1.0 / math.sqrt(HD)
    for j, (acc, factor) in enumerate(((acc0, scale), (acc1, scale), (acc2, 1.0))):
        low = (acc[...] * factor).astype(BF16)
        dqkv[:, j * W : (j + 1) * W] = low
        if j != 1:
            at = (j // 2) * W
            sm[6:7, at : at + W] = jnp.sum(low.astype(F32), 0, keepdims=True)

    @pl.loop(0, D // W)
    def _(j):
        da1s[:, tile(j)] = dot_nt(dqkv[...], wqkv[tile(j), :]).astype(BF16)

    start(ex[DA1])
    wgs[2][...] = dot_tn(att[...], dy1[...]).astype(BF16)

    @pl.loop(0, D // W)
    def _(j):
        wgs[3][tile(j), :] = dot_tn(a1[:, tile(j)], dqkv[...]).astype(BF16)

    arrive(ex[DA1])
    grad_u, gain_grad, shift_grad = norm_back(summed(da1s, da1r), xc[...], gains[0:1, :])
    sm[0:1, :] = gain_grad
    sm[2:3, :] = shift_grad
    low = (dx2c[...] + grad_u).astype(BF16)
    pipe_bs[...] = low
    dxg[mine, :] = low

    @pl.when(second)
    def _():
        back.start()

    start(ex[DX])
    smz[z] = sm[...]
    start(ex[SMALL])

    @pl.when(second)
    def _():
        down()
        layer_output()
        start(ex[OUT])

    if reduce_dp:
        steps = [bucket(b) for b in range(4)]
        for s in range(7):
            for b in range(4):
                steps[b][s]()

    arrive(ex[OUT])
    act_copy.start()
    arrive(ex[DX])
    dx_copy = pltpu.make_async_copy(dxg.at[pl.ds(0, USED)], dx_out, out_sem.at[1])
    dx_copy.start()

    arrive(ex[SMALL])
    whole = smz[0] + smz[1] + smz[2] + smz[3]
    own_rows = lax.broadcasted_iota(jnp.int32, (8, D), 0) >= 5
    whole = jnp.where(own_rows, sm[...], whole)
    if reduce_dp:
        smc[gc] = whole
        core_copy = sd_copy(0, smc.at[gc], smc.at[gc], core_peer)
        core_copy.start()
        core_copy.wait()
        smy[gy] = smc[0] + smc[1]
        y_copy = sd_copy(1, smy.at[gy], smy.at[gy], y_peer)
        y_copy.start()
        y_copy.wait()
        smx[gx] = smy[0] + smy[1]
        x_copies = [sd_copy(2 + i, smx.at[gx], smx.at[gx], x_peers[i]) for i in range(3)]
        start(x_copies)
        for copy in x_copies:
            copy.wait()
        whole = smx[0] + smx[1] + smx[2] + smx[3]
    small_out[...] = whole

    act_copy.wait()
    dx_copy.wait()
    for k in (Y1, A2, Y2, OUT, DA2, DY1, DA1, DX, SMALL):
        sent(ex[k])

    @pl.when(first)
    def _():
        forth.wait_send()
        sent(ex[DOUT])

    @pl.when(second)
    def _():
        back.wait_send()
        sent(ex[A1])

    if not reduce_dp:
        copies = [
            pltpu.make_async_copy(wg, out, dp_l.at[b, 0])
            for b, (wg, out) in enumerate(zip(wgs, gouts))
        ]
        start(copies)
        for copy in copies:
            copy.wait()


def call(reduce_dp, *operands):
    hbm = pl.BlockSpec(memory_space=pl.ANY)
    vmem = pl.BlockSpec(memory_space=pltpu.VMEM)
    smem = pl.BlockSpec(memory_space=pltpu.SMEM)

    def low(*shape):
        return pltpu.VMEM(shape, BF16)

    def wide(*shape):
        return pltpu.VMEM(shape, F32)

    scratch = [
        wide(PAD, D), wide(PAD, D), low(D, 768), low(256, D), low(D, D), low(D, D),
        wide(PAD, PAD), wide(CH, D), low(PAD, D), low(PAD, 768), wide(HEADS, PAD, PAD), low(PAD, W),
        low(PAD, D), low(3, CH, D), wide(CH, D), low(PAD, D), wide(PAD, D), low(PAD, D),
        low(PAD, D), low(3, CH, D), low(PAD, D), wide(CH, D), low(PAD, D), wide(PAD, D), low(PAD, D),
        low(PAD, D), low(3, CH, D), wide(CH, D), low(PAD, D), low(PAD, 768), low(PAD, D),
        low(3, CH, D), low(PAD, D),
        low(CH, D), low(CH, D), low(CH, D), low(CH, D),
        wide(8, D), wide(4, 8, D), wide(2, 8, D), wide(2, 8, D), wide(4, 8, D),
        wide(PAD, W), wide(PAD, W), wide(PAD, W),
    ]
    scratch += [low(size, width) for size, width, p, q in BUCKETS]
    scratch += [low(size // 2, width) for size, width, p, q in BUCKETS]
    scratch += [low(3, p // 4, width) for size, width, p, q in BUCKETS]
    scratch += [low(q // 2, width) for size, width, p, q in BUCKETS if q]
    scratch += [low(p // 8, width) for size, width, p, q in BUCKETS]
    scratch += [low(3, q // 8, width) for size, width, p, q in BUCKETS if q]
    dma = pltpu.SemaphoreType.DMA
    scratch += [
        dma((6,)), dma((2,)), dma((11, 3)), dma((11, 3)), dma((2,)), dma((2,)),
        dma((4, 18)), dma((4, 18)), dma((4, 2)), dma((5,)), dma((5,)),
    ]
    return pl.pallas_call(
        functools.partial(kernel, reduce_dp),
        out_shape=[
            jax.ShapeDtypeStruct((USED, D), BF16),
            jax.ShapeDtypeStruct((USED, D), BF16),
            *[jax.ShapeDtypeStruct((size, width), BF16) for size, width, _, _ in BUCKETS],
            jax.ShapeDtypeStruct((8, D), F32),
        ],
        in_specs=[hbm, hbm, smem, vmem, vmem, vmem, hbm, vmem, hbm, vmem, hbm, vmem, hbm],
        out_specs=[hbm] * 6 + [vmem],
        scratch_shapes=scratch,
        compiler_params=pltpu.CompilerParams(
            collective_id=0, has_side_effects=True, vmem_limit_bytes=60 * 1024 * 1024
        ),
        name="layers",
    )(*operands)


def local(
    tokens,
    cotangent,
    doc_lengths,
    live_mask,
    norm_gains,
    norm_biases,
    query_key_value,
    query_value_bias,
    output_weight,
    output_biases,
    expand_weight,
    expand_bias,
    reduce_weight,
):
    reduce_dp = lax.axis_size("dp") == 16
    act, dx, gdn, gup, go, gqkv, small = call(
        reduce_dp,
        tokens.reshape(USED, D),
        cotangent.reshape(USED, D),
        doc_lengths.reshape(SLOTS, 3),
        live_mask,
        norm_gains[0],
        norm_biases[0],
        query_key_value[0].reshape(D, 768),
        query_value_bias[0],
        output_weight[0],
        output_biases[0],
        expand_weight[0],
        expand_bias,
        reduce_weight[0],
    )
    return (
        act.astype(F32).reshape(1, SLOTS, ROWS, D),
        dx.astype(F32).reshape(1, SLOTS, ROWS, D),
        small[None, 0:2],
        small[None, 2:4],
        gqkv.astype(F32).reshape(1, D, 3, 256),
        small[6, 0:512].reshape(1, 2, 256),
        go.astype(F32)[None],
        small[None, 4:6],
        gup.astype(F32)[None],
        small[7:8],
        gdn.astype(F32)[None],
    )


def solution(mesh):
    in_specs = (
        P(None, "dp", None),
        P(None, "dp", None),
        P(None, "dp", None),
        P(None, "dp"),
        P("pipe", None, None),
        P("pipe", None, None),
        P("pipe", None, None, "tensor"),
        P("pipe", None, "tensor"),
        P("pipe", "tensor", None),
        P("pipe", None, None),
        P("pipe", None, "tensor"),
        P("pipe", "tensor"),
        P("pipe", "tensor", None),
    )
    out_specs = (
        P("pipe", None, "dp", None),
        P("pipe", None, "dp", None),
        P("pipe", None, None),
        P("pipe", None, None),
        P("pipe", None, None, "tensor"),
        P("pipe", None, "tensor"),
        P("pipe", "tensor", None),
        P("pipe", None, None),
        P("pipe", None, "tensor"),
        P("pipe", "tensor"),
        P("pipe", "tensor", None),
    )
    return jax.shard_map(local, mesh=mesh, in_specs=in_specs, out_specs=out_specs, check_vma=False)
```

time: 902 us -> 230 us (0.25); the launches traced: 890 us -> 229 us
  waiting for transfers between devices: 522 us -> 0 us
  Pallas kernels: 0 us -> 206 us
  matrix products: 136 us -> 0 us
  other arithmetic: 103 us -> 12 us
  blocking collectives: 53 us -> 0 us
  local copies, waits for them, and re-layouts: 39.2 us -> 9.77 us
  starting transfers between devices: 18.9 us -> 0 us
  between operations: 17.5 us -> 0.69 us
    psum x12 -> x0, waiting for transfers between devices: 515 us -> none  [the longest x4 162 us: forward_layer(): lax.psum(jnp.dot(attended, out_weight, preferred_element_type=jnp.float32...]
    pallas_call x0 -> x1, Pallas kernels: none -> 206 us  [call(): pl.pallas_call(functools.partial(kernel, reduce_dp), out_shape=[jax.Shape...]
    dot_general x76 -> x0, matrix products: 136 us -> none  [the longest x4 18.2 us: backward_feedforward(): jnp.einsum('rf,rd->fd', activated, grad_low, preferred_element_type=jnp.f...]
    reduce_sum x52 -> x0, other arithmetic: 61.5 us -> none  [the longest x16 22.4 us: layer_norm(): center = inputs - jnp.mean(inputs, -1, keepdims=True)]
    psum x1 -> x0, blocking collectives: 53 us -> none  [local(): lax.psum(gain_two.astype(jnp.bfloat16), 'dp').astype(jnp.float32)]
    ppermute x6 -> x0, starting transfers between devices: 18 us -> none  [from_behind(): return lax.ppermute(block, axis, route)]
    convert_element_type x25 -> x0, other arithmetic: 12.5 us -> none  [the longest x4 3.11 us: forward_layer(): queries = (projected[:, 0] + qv_bias[0]).astype(jnp.bfloat16)]
    convert_element_type x16 -> x0, local copies, waits for them, and re-layouts: 12 us -> none  [the longest x4 3.5 us: backward_attention(): grad_query = grad_query.reshape(row_count, -1).astype(jnp.bfloat16)]
  transfers between devices with their start and end apart: 18 -> 0, of which waited for: 15 -> 0; matrix products, arithmetic and copies ran while one was open for 10% -> 0% of each run, Pallas kernels for 0% -> 0%
where the time goes in v1:
time: 230 us; the launch traced here: 229 us
  Pallas kernels  206 us (90%)
  other arithmetic  12 us (5%)
  local copies, waits for them, and re-layouts  9.77 us (4%)
    pallas_call x1, Pallas kernels, call(): pl.pallas_call(functools.partial(kernel, reduce_dp), out_shape=[jax.Shape...  206 us
    broadcast_in_dim x1, other arithmetic, local(): gdn.astype(F32)[None]  6.67 us
    unnamed x9, local copies, waits for them, and re-layouts  4.67 us

profile of v1, /device:TPU:1, one launch (start us, length us, event | category | flops | bytes accessed | tf_op | source)
XLA Modules:
  0.0 228.7 jit_solution(9610206697842400169)
XLA Ops:
  0.6 1.7 copy.26
  2.4 0.0 copy-start.2
  2.4 1.6 copy.27.wqkv_hbm
  3.9 0.0 copy-done.2
  4.0 0.6 copy.32
  4.5 206.3 %layers.1 = (bf16[240,1024]{1,0:T(8,128)(2,1)}, bf16[240,1024]{1,0:T(8,128)(2,1)}, bf16[1024,1024]{1,0:T(8,128)(2,1)}, bf16[1024,1024]{1,0:T(8,128)(2,1)}, bf16[...) custom-call(f32[240,1024]{1,0:T(8,128)} %bitcast.37, f32[240,1024]{1,0:T(8,128)} %bitcast.38, ...), custom_call_target="tpu_custom_call" | custom-call | tf_op jit(solution)/shard_map/layers/pallas_call | solution.py:614
  210.8 0.0 copy-start.1
  210.9 6.7 %bitcast_convert_fusion = (f32[1,1024,1024]{2,1,0:T(8,128)}, f32[1,1024,1024]{2,1,0:T(8,128)}) fusion(bf16[1024,1024]{1,0:T(8,128)(2,1)} %get-tuple-element.24, bf16[1024,1024]{1,0:T(8,128)(2,1)} %get-tuple-element.23), kind=kLoop, calls=%fused_computation | loop fusion | flops 2097152 | bytes 12582912 | tf_op jit(solution)/shard_map/broadcast_in_dim | solution.py:675
  217.5 0.0 copy-done.1
  217.5 0.6 slice_bitcast_fusion
  218.2 0.6 reshape_squeeze.7
  218.8 0.6 slice.19
  219.3 1.7 copy.28
  221.1 2.4 %copy.29 = f32[1,1024,3,256]{3,1,2,0:T(8,128)} copy(f32[1,1024,3,256]{1,3,2,0:T(8,128)S(1)} %bitcast.33) | data formatting | bytes 6291456
  223.4 0.0 copy-start
  223.4 2.2 bitcast_convert_fusion.2
  225.6 2.1 convert.6
  227.7 0.0 copy-done
  227.7 1.1 convert.7
  (1 shorter events, 0.0 us)
Async XLA Ops:
  2.4 1.6 copy-start.2
  210.8 6.7 %copy-start.1 = (f32[8,1024]{1,0:T(8,128)S(1)}, f32[8,1024]{1,0:T(8,128)}, u32[]{:S(2)}) copy-start(f32[8,1024]{1,0:T(8,128)} %get-tuple-element.20) | copy-start | bytes 98308
  223.4 4.3 %copy-start = (bf16[240,1024]{1,0:T(8,128)(2,1)S(1)}, bf16[240,1024]{1,0:T(8,128)(2,1)}, u32[]{:S(2)}) copy-start(bf16[240,1024]{1,0:T(8,128)(2,1)} %get-tuple-element.19) | copy-start | bytes 1474564

commit v2 on v1

--- a/solution.py
+++ b/solution.py
@@ -21,7 +21,8 @@
 HEADS = 4
 HD = 64
 W = 256
-BUCKETS = ((1024, 1024, 256, 256), (1024, 1024, 256, 256), (256, 1024, 128, 0), (1024, 768, 256, 256))
+BLOCKS = (slice(0, 512), slice(512, 1024))
+BUCKETS = ((1024, 1024, 256, 256), (1024, 1024, 256, 256), (256, 1024, 128, 0), (3072, 256, 768, 768))
 A1, Y1, A2, Y2, OUT, DOUT, DA2, DY1, DA1, DX, SMALL = range(11)
 
 
@@ -61,7 +62,7 @@
     act_out, dx_out, gdn_out, gup_out, go_out, gqkv_out, small_out,
     tok, cot, wqkv, wo, wup, wdn, mask, xc, a1, qkv, prob, att, y1s, y1r, x2c, a2, slope, g,
     y2s, y2r, actg, doc, dy2, dg, dh, da2s, da2r, dx2c, dy1, dqkv, da1s, da1r, dxg,
-    pipe_f, pipe_b, pipe_fs, pipe_bs, sm, smz, smc, smy, smx, acc0, acc1, acc2,
+    pipe_f, pipe_b, pipe_fs, pipe_bs, sm, smz, smc, smy, smx,
     wg0, wg1, wg2, wg3, rc0, rc1, rc2, rc3, p10, p11, p12, p13, q10, q11, q13,
     p20, p21, p22, p23, q20, q21, q23,
     load_sem, out_sem, tp_s, tp_r, pp_s, pp_r, dp_s, dp_r, dp_l, sd_s, sd_r,
@@ -92,8 +93,16 @@
         "up": load(4, wup_hbm, wup),
         "dn": load(5, wdn_hbm, wdn),
     }
-    for name in ("tok", "cot", "qkv", "o", "up", "dn"):
-        loads[name].start()
+
+    @pl.when(first)
+    def _():
+        for name in ("tok", "qkv", "o", "up", "dn"):
+            loads[name].start()
+
+    @pl.when(second)
+    def _():
+        for name in ("cot", "dn", "qkv", "o", "up"):
+            loads[name].start()
 
     barrier = pltpu.get_barrier_semaphore()
     partners = [{"tensor": (z + t) % 4} for t in (1, 2, 3)] + [{"pipe": 1 - pipe}]
@@ -194,7 +203,7 @@
         return pl.ds(pl.multiple_of(at, 16), size)
 
     def add_into(dst, at, size, terms):
-        step = min(size, 64)
+        step = next(n for n in (64, 48, 32, 16) if size % n == 0)
 
         @pl.loop(0, size // step)
         def _(i):
@@ -311,6 +320,12 @@
             device_id={"dp": peer}, device_id_type=MESH,
         )
 
+    steps = [bucket(b) for b in range(4)] if reduce_dp else None
+
+    def early(b, s):
+        if reduce_dp:
+            pl.when(first)(steps[b][s])
+
     @pl.when(first)
     def _():
         loads["tok"].wait()
@@ -322,13 +337,10 @@
             a1[tile(i, CH), :] = (unit * gains[0:1, :] + shifts[0:1, :]).astype(BF16)
 
         xc[...] = tok[mine, :]
-        loads["cot"].wait()
-        loads["dn"].wait()
 
     def output_grads():
-        @pl.loop(0, D // W)
-        def _(j):
-            dg[:, tile(j)] = dot_nt(dy2[...], wdn[tile(j), :])
+        for j in BLOCKS:
+            dg[:, j] = dot_nt(dy2[...], wdn[j, :])
 
     @pl.when(second)
     def _():
@@ -341,7 +353,6 @@
         doc[...] = cot[mine, :]
         loads["dn"].wait()
         output_grads()
-        loads["tok"].wait()
         forth.wait_recv()
         inputs = pipe_f[...].astype(F32)
         xc[...] = inputs
@@ -352,7 +363,7 @@
 
     loads["qkv"].wait()
     for j in range(3):
-        part = dot_nn(a1[...], wqkv[:, j * W : (j + 1) * W])
+        part = dot_nn(a1[...], wqkv[j])
         if j != 1:
             part = part + qvb[j // 2 : j // 2 + 1, :]
         qkv[:, j * W : (j + 1) * W] = part.astype(BF16)
@@ -360,23 +371,19 @@
     def head_rows(values, h):
         return (values.astype(F32) * jnp.where(head_of == h, 1.0, 0.0)).astype(BF16)
 
-    acc0[...] = jnp.zeros_like(acc0)
-
-    @pl.loop(0, HEADS)
-    def _(h):
+    attended = jnp.zeros((PAD, W), F32)
+    for h in range(HEADS):
         scores = dot_nt(head_rows(qkv[:, 0:W], h), qkv[:, W : 2 * W]) * (1.0 / math.sqrt(HD))
         scores = jnp.where(mask[...] > 0.5, scores, -1000000000.0)
         expo = jnp.exp(scores - jnp.max(scores, -1, keepdims=True))
         p = expo / jnp.sum(expo, -1, keepdims=True)
         prob[h] = p
-        acc0[...] += dot_nn(p.astype(BF16), head_rows(qkv[:, 2 * W : 3 * W], h))
-
-    att[...] = acc0[...].astype(BF16)
+        attended = attended + dot_nn(p.astype(BF16), head_rows(qkv[:, 2 * W : 3 * W], h))
+
+    att[...] = attended.astype(BF16)
     loads["o"].wait()
-
-    @pl.loop(0, D // W)
-    def _(j):
-        y1s[:, tile(j)] = dot_nn(att[...], wo[:, tile(j)]).astype(BF16)
+    for j in BLOCKS:
+        y1s[:, j] = dot_nn(att[...], wo[:, j]).astype(BF16)
 
     start(ex[Y1])
     arrive(ex[Y1])
@@ -388,21 +395,19 @@
     loads["up"].wait()
     arrive(ex[A2])
 
-    @pl.loop(0, D // W)
-    def _(j):
-        hidden = dot_nn(a2[...], wup[:, tile(j)]) + upb[:, tile(j)]
+    for j in BLOCKS:
+        hidden = dot_nn(a2[...], wup[:, j]) + upb[:, j]
         square = hidden * hidden
         root = math.sqrt(2.0 / math.pi)
         bent = jnp.tanh(root * hidden * (1.0 + 0.044715 * square))
         lifted = 0.5 * (1.0 + bent)
-        g[:, tile(j)] = (hidden * lifted).astype(BF16)
+        g[:, j] = (hidden * lifted).astype(BF16)
         inner = root * (1.0 + 3.0 * 0.044715 * square)
-        slope[:, tile(j)] = lifted + 0.5 * hidden * (1.0 - bent * bent) * inner
+        slope[:, j] = lifted + 0.5 * hidden * (1.0 - bent * bent) * inner
 
     def down():
-        @pl.loop(0, D // W)
-        def _(j):
-            y2s[:, tile(j)] = dot_nn(g[...], wdn[:, tile(j)]).astype(BF16)
+        for j in BLOCKS:
+            y2s[:, j] = dot_nn(g[...], wdn[:, j]).astype(BF16)
 
         start(ex[Y2])
 
@@ -416,6 +421,7 @@
 
     @pl.when(first)
     def _():
+        loads["dn"].wait()
         down()
         layer_output()
         forth.start()
@@ -427,15 +433,13 @@
         arrive(ex[DOUT])
         output_grads()
 
-    @pl.loop(0, D // W)
-    def _(j):
-        grad = (dg[:, tile(j)] * slope[:, tile(j)]).astype(BF16)
-        dh[:, tile(j)] = grad
-        sm[7:8, tile(j)] = jnp.sum(grad.astype(F32), 0, keepdims=True)
-
-    @pl.loop(0, D // W)
-    def _(j):
-        da2s[:, tile(j)] = dot_nt(dh[...], wup[tile(j), :]).astype(BF16)
+    for j in BLOCKS:
+        grad = (dg[:, j] * slope[:, j]).astype(BF16)
+        dh[:, j] = grad
+        sm[7:8, j] = jnp.sum(grad.astype(F32), 0, keepdims=True)
+
+    for j in BLOCKS:
+        da2s[:, j] = dot_nt(dh[...], wup[j, :]).astype(BF16)
 
     start(ex[DA2])
 
@@ -443,61 +447,62 @@
     def _():
         sm[5:6, :] = jnp.sum(dy2[...].astype(F32), 0, keepdims=True)
 
-    @pl.loop(0, D // W)
-    def _(j):
-        wgs[0][tile(j), :] = dot_tn(g[:, tile(j)], dy2[...]).astype(BF16)
-
-    @pl.loop(0, D // W)
-    def _(j):
-        wgs[1][tile(j), :] = dot_tn(a2[:, tile(j)], dh[...]).astype(BF16)
-
+    for j in BLOCKS:
+        wg0[j, :] = dot_tn(g[:, j], dy2[...]).astype(BF16)
+
+    early(0, 0)
+    for j in BLOCKS:
+        wg1[j, :] = dot_tn(a2[:, j], dh[...]).astype(BF16)
+
+    early(1, 0)
     arrive(ex[DA2])
     grad_u, gain_grad, shift_grad = norm_back(summed(da2s, da2r), x2c[...], gains[1:2, :])
     grad_middle = doc[...] + grad_u
+    dy1[mine, :] = grad_middle.astype(BF16)
+    start(ex[DY1])
     dx2c[...] = grad_middle
     sm[1:2, :] = gain_grad
     sm[3:4, :] = shift_grad
     sm[4:5, :] = jnp.sum(grad_middle, 0, keepdims=True)
-    dy1[mine, :] = grad_middle.astype(BF16)
-    start(ex[DY1])
+    early(0, 1)
     arrive(ex[DY1])
 
     att_grad = dot_nt(dy1[...], wo[...]).astype(BF16)
     dqkv[:, 2 * W : 3 * W] = att_grad
-    acc0[...] = jnp.zeros_like(acc0)
-    acc1[...] = jnp.zeros_like(acc1)
-    acc2[...] = jnp.zeros_like(acc2)
-
-    @pl.loop(0, HEADS)
-    def _(h):
+    grad_q = grad_k = grad_v = jnp.zeros((PAD, W), F32)
+    for h in range(HEADS):
         p = prob[h]
         own = head_rows(dqkv[:, 2 * W : 3 * W], h)
         grad_p = dot_nt(own, qkv[:, 2 * W : 3 * W])
-        acc2[...] += dot_tn(p.astype(BF16), own)
+        grad_v = grad_v + dot_tn(p.astype(BF16), own)
         grad_s = p * (grad_p - jnp.sum(grad_p * p, -1, keepdims=True))
         grad_s = grad_s.astype(BF16)
-        acc0[...] += dot_nn(grad_s, head_rows(qkv[:, W : 2 * W], h))
-        acc1[...] += dot_tn(grad_s, head_rows(qkv[:, 0:W], h))
+        grad_q = grad_q + dot_nn(grad_s, head_rows(qkv[:, W : 2 * W], h))
+        grad_k = grad_k + dot_tn(grad_s, head_rows(qkv[:, 0:W], h))
 
     scale = 1.0 / math.sqrt(HD)
-    for j, (acc, factor) in enumerate(((acc0, scale), (acc1, scale), (acc2, 1.0))):
-        low = (acc[...] * factor).astype(BF16)
+    for j, (grad, factor) in enumerate(((grad_q, scale), (grad_k, scale), (grad_v, 1.0))):
+        low = (grad * factor).astype(BF16)
         dqkv[:, j * W : (j + 1) * W] = low
         if j != 1:
             at = (j // 2) * W
             sm[6:7, at : at + W] = jnp.sum(low.astype(F32), 0, keepdims=True)
 
-    @pl.loop(0, D // W)
-    def _(j):
-        da1s[:, tile(j)] = dot_nt(dqkv[...], wqkv[tile(j), :]).astype(BF16)
+    for j in BLOCKS:
+        part = dot_nt(dqkv[:, 0:W], wqkv[0, j, :]) + dot_nt(dqkv[:, W : 2 * W], wqkv[1, j, :])
+        da1s[:, j] = (part + dot_nt(dqkv[:, 2 * W : 3 * W], wqkv[2, j, :])).astype(BF16)
 
     start(ex[DA1])
-    wgs[2][...] = dot_tn(att[...], dy1[...]).astype(BF16)
-
-    @pl.loop(0, D // W)
-    def _(j):
-        wgs[3][tile(j), :] = dot_tn(a1[:, tile(j)], dqkv[...]).astype(BF16)
-
+    wg2[...] = dot_tn(att[...], dy1[...]).astype(BF16)
+    early(2, 0)
+    for j in range(D // W):
+        part = dot_tn(a1[:, j * W : (j + 1) * W], dqkv[...]).astype(BF16)
+        for i in range(3):
+            at = i * D + j * W
+            wg3[at : at + W, :] = part[:, i * W : (i + 1) * W]
+
+    early(3, 0)
+    early(1, 1)
     arrive(ex[DA1])
     grad_u, gain_grad, shift_grad = norm_back(summed(da1s, da1r), xc[...], gains[0:1, :])
     sm[0:1, :] = gain_grad
@@ -521,10 +526,27 @@
         start(ex[OUT])
 
     if reduce_dp:
-        steps = [bucket(b) for b in range(4)]
-        for s in range(7):
-            for b in range(4):
+        early(0, 2)
+        early(2, 1)
+        early(3, 1)
+        early(1, 2)
+
+        @pl.when(first)
+        def _():
+            for b, s in ((0, 3), (2, 2), (3, 2), (1, 3), (0, 4), (2, 3), (3, 3), (1, 4)):
                 steps[b][s]()
+
+        @pl.when(second)
+        def _():
+            for s in range(5):
+                for b in range(4):
+                    if s < 4 or b < 2:
+                        steps[b][s]()
+
+        for b, s in ((0, 5), (2, 4), (3, 4), (1, 5), (2, 5), (3, 5)):
+            steps[b][s]()
+        for b in range(4):
+            steps[b][6]()
 
     arrive(ex[OUT])
     act_copy.start()
@@ -590,7 +612,7 @@
         return pltpu.VMEM(shape, F32)
 
     scratch = [
-        wide(PAD, D), wide(PAD, D), low(D, 768), low(256, D), low(D, D), low(D, D),
+        wide(PAD, D), wide(PAD, D), low(3, D, W), low(256, D), low(D, D), low(D, D),
         wide(PAD, PAD), wide(CH, D), low(PAD, D), low(PAD, 768), wide(HEADS, PAD, PAD), low(PAD, W),
         low(PAD, D), low(3, CH, D), wide(CH, D), low(PAD, D), wide(PAD, D), low(PAD, D),
         low(PAD, D), low(3, CH, D), low(PAD, D), wide(CH, D), low(PAD, D), wide(PAD, D), low(PAD, D),
@@ -598,7 +620,6 @@
         low(3, CH, D), low(PAD, D),
         low(CH, D), low(CH, D), low(CH, D), low(CH, D),
         wide(8, D), wide(4, 8, D), wide(2, 8, D), wide(2, 8, D), wide(4, 8, D),
-        wide(PAD, W), wide(PAD, W), wide(PAD, W),
     ]
     scratch += [low(size, width) for size, width, p, q in BUCKETS]
     scratch += [low(size // 2, width) for size, width, p, q in BUCKETS]
@@ -623,10 +644,48 @@
         out_specs=[hbm] * 6 + [vmem],
         scratch_shapes=scratch,
         compiler_params=pltpu.CompilerParams(
-            collective_id=0, has_side_effects=True, vmem_limit_bytes=60 * 1024 * 1024
+            collective_id=0, has_side_effects=True, vmem_limit_bytes=40 * 1024 * 1024
         ),
         name="layers",
     )(*operands)
+
+
+def widen_kernel(*refs):
+    small, lows = refs[6], refs[:6]
+    outs, (gains, shifts, qv, biases, upb) = refs[7:13], refs[13:]
+    for low, out in zip(lows, outs):
+        out[...] = low[...].astype(F32)
+    gains[...] = small[0:2, :]
+    shifts[...] = small[2:4, :]
+    biases[...] = small[4:6, :]
+    qv[0:1, :] = small[6:7, 0:W]
+    qv[1:2, :] = small[6:7, W : 2 * W]
+    upb[...] = small[7:8, :]
+
+
+def widen(lows, small):
+    count = 8
+
+    def spec(shape):
+        blocks = 5 if shape[0] == USED else count
+        return pl.BlockSpec(
+            (shape[0] // blocks, shape[1]), lambda i: (jnp.minimum(i, blocks - 1), 0)
+        )
+
+    def fixed(shape):
+        return pl.BlockSpec(shape, lambda i: (0, 0))
+
+    flat = [(2, D), (2, D), (2, W), (2, D), (1, D)]
+    return pl.pallas_call(
+        widen_kernel,
+        grid=(count,),
+        out_shape=[jax.ShapeDtypeStruct(a.shape, F32) for a in lows]
+        + [jax.ShapeDtypeStruct(shape, F32) for shape in flat],
+        in_specs=[spec(a.shape) for a in lows] + [fixed((8, D))],
+        out_specs=[spec(a.shape) for a in lows] + [fixed(shape) for shape in flat],
+        compiler_params=pltpu.CompilerParams(vmem_limit_bytes=40 * 1024 * 1024),
+        name="widen",
+    )(*lows, small)
 
 
 def local(
@@ -653,7 +712,7 @@
         live_mask,
         norm_gains[0],
         norm_biases[0],
-        query_key_value[0].reshape(D, 768),
+        query_key_value[0].transpose(1, 0, 2),
         query_value_bias[0],
         output_weight[0],
         output_biases[0],
@@ -661,18 +720,21 @@
         expand_bias,
         reduce_weight[0],
     )
+    act, dx, gdn, gup, go, gqkv, gains, shifts, qv, biases, upb = widen(
+        (act, dx, gdn, gup, go, gqkv), small
+    )
     return (
-        act.astype(F32).reshape(1, SLOTS, ROWS, D),
-        dx.astype(F32).reshape(1, SLOTS, ROWS, D),
-        small[None, 0:2],
-        small[None, 2:4],
-        gqkv.astype(F32).reshape(1, D, 3, 256),
-        small[6, 0:512].reshape(1, 2, 256),
-        go.astype(F32)[None],
-        small[None, 4:6],
-        gup.astype(F32)[None],
-        small[7:8],
-        gdn.astype(F32)[None],
+        act.reshape(1, SLOTS, ROWS, D),
+        dx.reshape(1, SLOTS, ROWS, D),
+        gains[None],
+        shifts[None],
+        gqkv.reshape(3, D, W).transpose(1, 0, 2)[None],
+        qv[None],
+        go[None],
+        biases[None],
+        gup[None],
+        upb,
+        gdn[None],
     )
 
 

time: 230 us -> 200 us (0.87)
  Pallas kernels: 206 us -> 187 us
  other arithmetic: 12 us -> 0 us
    pallas_call x1, Pallas kernels: 206 us -> 181 us  [call(): pl.pallas_call(functools.partial(kernel, reduce_dp), out_shape=[jax.Shape...]
    broadcast_in_dim x2 -> x0, other arithmetic: 8.85 us -> none  [the longest x1 6.67 us: local(): gdn.astype(F32)[None]]
    unnamed x9 -> x23, local copies, waits for them, and re-layouts: 4.67 us -> 11.3 us
    pallas_call x0 -> x1, Pallas kernels: none -> 5.91 us  [widen(): pl.pallas_call(widen_kernel, grid=(count,), out_shape=[jax.ShapeDtypeStru...]
    reshape x2 -> x0, other arithmetic: 3.13 us -> none  [the longest x1 2.08 us: local(): act.astype(F32).reshape(1, SLOTS, ROWS, D)]
where the time goes in v2:
time: 200 us; the launch traced here: 199 us
  Pallas kernels  187 us (94%)
  local copies, waits for them, and re-layouts  11.3 us (6%)
    pallas_call x1, Pallas kernels, call(): pl.pallas_call(functools.partial(kernel, reduce_dp), out_shape=[jax.Shape...  181 us
    unnamed x23, local copies, waits for them, and re-layouts  11.3 us
    pallas_call x1, Pallas kernels, widen(): pl.pallas_call(widen_kernel, grid=(count,), out_shape=[jax.ShapeDtypeStru...  5.91 us

profile of v2, /device:TPU:1, one launch (start us, length us, event | category | flops | bytes accessed | tf_op | source)
XLA Modules:
  0.0 198.5 jit_solution(13255461189505934360)
XLA Ops:
  0.6 0.7 copy.26
  1.3 0.0 copy-start
  1.3 1.6 copy-done
  2.9 0.0 copy-start.1
  2.9 1.4 copy-done.1
  4.3 0.0 copy-start.2
  4.3 1.2 copy-done.2
  5.5 0.0 copy-start.3
  5.5 1.2 copy-done.3
  6.7 0.0 copy-start.4
  6.7 1.0 copy-done.4
  7.8 0.0 copy-start.5
  7.8 0.7 copy-done.5
  8.5 0.7 copy-done.6
  9.2 0.0 copy-start.7
  9.2 0.7 copy-done.7
  9.9 0.0 copy-start.8
  9.9 0.7 copy-done.8
  10.6 0.0 copy-start.9
  10.6 0.7 copy-done.9
  11.2 0.0 copy-start.10
  11.2 0.7 copy-done.10
  11.9 180.7 %layers.1 = (bf16[240,1024]{1,0:T(8,128)(2,1)S(1)}, bf16[240,1024]{1,0:T(8,128)(2,1)S(1)}, bf16[1024,1024]{1,0:T(8,128)(2,1)S(1)}, bf16[1024,1024]{1,0:T(8,128)(...) custom-call(f32[240,1024]{1,0:T(8,128)S(1)} %bitcast.31, ...), custom_call_target="tpu_custom_call" | custom-call | tf_op jit(solution)/shard_map/layers/pallas_call | solution.py:635
  192.6 5.9 %widen.1 = (f32[240,1024]{1,0:T(8,128)}, f32[240,1024]{1,0:T(8,128)}, f32[1024,1024]{1,0:T(8,128)}, f32[1024,1024]{1,0:T(8,128)}, f32[256,1024]{1,0:T(8,128)}, /...) custom-call(bf16[240,1024]{1,0:T(8,128)(2,1)S(1)} %get-tuple-element, ...), custom_call_target="tpu_custom_call" | custom-call | tf_op jit(solution)/shard_map/widen/pallas_call | solution.py:679
  (1 shorter events, 0.0 us)
Async XLA Ops:
  1.3 1.6 copy-start
  2.9 1.4 copy-start.1
  4.3 1.2 copy-start.2
  5.5 1.2 copy-start.3
  6.7 1.0 copy-start.4
  7.8 0.7 copy-start.5
  8.5 0.7 copy-start.6
  9.2 0.7 copy-start.7
  9.9 0.7 copy-start.8
  10.6 0.7 copy-start.9
  11.2 0.7 copy-start.10

commit v3 on v2

--- a/solution.py
+++ b/solution.py
@@ -22,7 +22,12 @@
 HD = 64
 W = 256
 BLOCKS = (slice(0, 512), slice(512, 1024))
-BUCKETS = ((1024, 1024, 256, 256), (1024, 1024, 256, 256), (256, 1024, 128, 0), (3072, 256, 768, 768))
+BUCKETS = (
+    (1024, 1024, (256, 128, 128)),
+    (1024, 1024, (128, 256, 128)),
+    (256, 1024, (0, 0, 128)),
+    (3072, 256, (512, 512, 512)),
+)
 A1, Y1, A2, Y2, OUT, DOUT, DA2, DY1, DA1, DX, SMALL = range(11)
 
 
@@ -58,18 +63,18 @@
 
 def kernel(
     reduce_dp,
-    tok_hbm, cot_hbm, docs, live, gains, shifts, wqkv_hbm, qvb, wo_hbm, obias, wup_hbm, upb, wdn_hbm,
+    tok_hbm, cot_hbm, docs, live_hbm, gains_hbm, shifts_hbm, wqkv_hbm, qvb_hbm, wo_hbm, obias_hbm,
+    wup_hbm, upb_hbm, wdn_hbm,
     act_out, dx_out, gdn_out, gup_out, go_out, gqkv_out, small_out,
     tok, cot, wqkv, wo, wup, wdn, mask, xc, a1, qkv, prob, att, y1s, y1r, x2c, a2, slope, g,
     y2s, y2r, actg, doc, dy2, dg, dh, da2s, da2r, dx2c, dy1, dqkv, da1s, da1r, dxg,
     pipe_f, pipe_b, pipe_fs, pipe_bs, sm, smz, smc, smy, smx,
-    wg0, wg1, wg2, wg3, rc0, rc1, rc2, rc3, p10, p11, p12, p13, q10, q11, q13,
-    p20, p21, p22, p23, q20, q21, q23,
+    wg0, wg1, wg2, wg3, rc0, rc1, rc2, rc3, in0, in1, in2, in3,
+    live, gains, shifts, qvb, obias, upb,
     load_sem, out_sem, tp_s, tp_r, pp_s, pp_r, dp_s, dp_r, dp_l, sd_s, sd_r,
 ):
     wgs, rcs = (wg0, wg1, wg2, wg3), (rc0, rc1, rc2, rc3)
-    p1s, q1s = (p10, p11, p12, p13), (q10, q11, None, q13)
-    p2s, q2s = (p20, p21, p22, p23), (q20, q21, None, q23)
+    ins = (in0, in1, in2, in3)
     gouts = (gdn_out, gup_out, go_out, gqkv_out)
     pipe = lax.axis_index("pipe")
     dp = lax.axis_index("dp")
@@ -81,6 +86,12 @@
     y_peer = gx * 4 + (1 - gy) * 2 + gc
     x_peers = [((gx + t) % 4) * 4 + gy * 2 + gc for t in (1, 2, 3)]
     mine = tile(z, CH)
+    cube_bits = (((gx + 1) // 2) % 2, gx // 2, gy)
+    cube_peers = (
+        (gx + 1 - 2 * (gx % 2)) * 4 + gy * 2 + gc,
+        (3 - gx) * 4 + gy * 2 + gc,
+        y_peer,
+    )
 
     def load(k, src, dst):
         return pltpu.make_async_copy(src, dst, load_sem.at[k])
@@ -93,6 +104,16 @@
         "up": load(4, wup_hbm, wup),
         "dn": load(5, wdn_hbm, wdn),
     }
+
+    small_loads = [
+        load(6 + k, src, dst)
+        for k, (src, dst) in enumerate((
+            (live_hbm, live), (gains_hbm, gains), (shifts_hbm, shifts),
+            (qvb_hbm, qvb), (obias_hbm, obias), (upb_hbm, upb),
+        ))
+    ]
+    for copy in small_loads:
+        copy.start()
 
     @pl.when(first)
     def _():
@@ -121,11 +142,13 @@
         for s in range(SLOTS):
             end = jnp.int32(0)
             for k in range(3):
-                end = end + docs[s, k]
+                end = end + docs[s, 0, k]
                 segment = segment + jnp.where((slot == s) & (spot >= end), 1, 0)
             alive = jnp.where((slot == s) & (spot.astype(F32) < counts[s : s + 1, :]), 1.0, alive)
         return at, segment, alive
 
+    for copy in small_loads:
+        copy.wait()
     counts = jnp.sum(live[...].astype(F32), 1, keepdims=True)
     row_at, row_segment, row_live = places((PAD, 1), 0)
     col_at, col_segment, col_live = places((1, PAD), 1)
@@ -202,117 +225,94 @@
     def rows(at, size):
         return pl.ds(pl.multiple_of(at, 16), size)
 
-    def add_into(dst, at, size, terms):
+    def add_into(dst, at, size, term):
         step = next(n for n in (64, 48, 32, 16) if size % n == 0)
 
         @pl.loop(0, size // step)
         def _(i):
             off = pl.multiple_of(i * step, 16)
-            total = dst[rows(at + off, step), :].astype(F32)
-            for term in terms:
-                total = total + term(off, step).astype(F32)
+            total = dst[rows(at + off, step), :].astype(F32) + term(off, step).astype(F32)
             dst[rows(at + off, step), :] = total.astype(BF16)
 
     def bucket(b):
-        size, _, p, q = BUCKETS[b]
+        size, _, parts = BUCKETS[b]
         half = size // 2
-        wg, rc, out = wgs[b], rcs[b], gouts[b]
-        p1, q1, p2, q2 = p1s[b], q1s[b], p2s[b], q2s[b]
+        wg, rc, inc, out = wgs[b], rcs[b], ins[b], gouts[b]
         base = gc * half
-        p8, p4, q8, q2n = p // 8, p // 4, q // 8, q // 2
-        c = {}
-        c["core"] = [dp_copy(b, 0, wg.at[rows((1 - gc) * half, half)], rc, core_peer)]
-        xs = [(gx + t) % 4 for t in (1, 2, 3)]
-        order = (1, 0, 2)
-        c["p1"] = [
-            dp_copy(b, 1 + i, rc.at[rows(xs[i] * p4, p4)], p1.at[i], x_peers[i]) for i in order
-        ]
-        p_fin = gx * p4 + gy * p8
-        c["p2"] = [dp_copy(b, 5, rc.at[rows(gx * p4 + (1 - gy) * p8, p8)], p2, y_peer)]
-        c["p3"] = [dp_copy(b, 9, rc.at[rows(p_fin, p8)], out.at[rows(base + p_fin, p8)], y_peer)]
-        p_part = out.at[rows(base + gx * p4, p4)]
-        c["p4"] = [dp_copy(b, 13 + i, p_part, p_part, x_peers[i]) for i in order]
-        half_out = out.at[rows(base, half)]
-        c["all"] = [dp_copy(b, 17, half_out, half_out, core_peer)]
-        keep = [
-            pltpu.make_async_copy(
-                rc.at[rows(p_fin, p8)], out.at[rows(base + p_fin, p8)], dp_l.at[b, 0]
+        whole = rows((1 - gc) * half, half)
+        core = dp_copy(b, 0, wg.at[whole], rc, core_peer)
+        pieces = []
+        for part, count in enumerate(parts):
+            if not count:
+                continue
+            at = sum(parts[:part])
+            begin, spare, size = at, at * 7 // 8, count
+            down, up = [], []
+            for step in range(3):
+                link = (part + step) % 3
+                bit, peer = cube_bits[link], cube_peers[link]
+                size = size // 2
+                own = begin + bit * size
+                copy = dp_copy(
+                    b, 1 + part * 6 + step, rc.at[rows(begin + (1 - bit) * size, size)],
+                    inc.at[rows(spare, size)], peer,
+                )
+                down.append((copy, own, size, spare))
+                here = out.at[rows(base + own, size)]
+                source = rc.at[rows(own, size)] if step == 2 else here
+                up.append(dp_copy(b, 4 + part * 6 + step, source, here, peer))
+                begin, spare = own, spare + size
+            keep = pltpu.make_async_copy(
+                rc.at[rows(begin, size)], out.at[rows(base + begin, size)], dp_l.at[b, part]
             )
-        ]
-        if q:
-            q_fin = p + gy * q2n + gx * q8
-            c["q1"] = [dp_copy(b, 4, rc.at[rows(p + (1 - gy) * q2n, q2n)], q1, y_peer)]
-            c["q2"] = [
-                dp_copy(b, 6 + i, rc.at[rows(p + gy * q2n + xs[i] * q8, q8)], q2.at[i], x_peers[i])
-                for i in order
-            ]
-            c["q3"] = [
-                dp_copy(b, 10 + i, rc.at[rows(q_fin, q8)], out.at[rows(base + q_fin, q8)], x_peers[i])
-                for i in order
-            ]
-            q_part = out.at[rows(base + p + gy * q2n, q2n)]
-            c["q4"] = [dp_copy(b, 16, q_part, q_part, y_peer)]
-            keep.append(
-                pltpu.make_async_copy(
-                    rc.at[rows(q_fin, q8)], out.at[rows(base + q_fin, q8)], dp_l.at[b, 1]
-                )
-            )
+            there = out.at[rows(base + at, count)]
+            last = dp_copy(b, 19 + part, there, there, core_peer)
+            pieces.append((at, count, down, up, keep, last))
 
         def step0():
-            start(c["core"])
+            core.start()
 
         def step1():
-            arrive(c["core"])
-            add_into(rc, 0, half, [lambda o, n: wg[rows(base + o, n), :]])
-            start(c["p1"])
-            if q:
-                start(c["q1"])
-
-        def step2():
-            if q:
-                arrive(c["q1"])
-                add_into(rc, p + gy * q2n, q2n, [lambda o, n: q1[rows(o, n), :]])
-                start(c["q2"])
-            arrive(c["p1"])
-            add_into(rc, gx * p4, p4, [
-                (lambda o, n, i=i: p1[i, rows(o, n), :]) for i in range(3)
-            ])
-            start(c["p2"])
-
-        def step3():
-            arrive(c["p2"])
-            add_into(rc, p_fin, p8, [lambda o, n: p2[rows(o, n), :]])
-            start(c["p3"])
-            keep[0].start()
-            if q:
-                arrive(c["q2"])
-                add_into(rc, q_fin, q8, [
-                    (lambda o, n, i=i: q2[i, rows(o, n), :]) for i in range(3)
-                ])
-                start(c["q3"])
-                keep[1].start()
-
-        def step4():
-            keep[0].wait()
-            arrive(c["p3"])
-            start(c["p4"])
-            if q:
-                keep[1].wait()
-                arrive(c["q3"])
-                start(c["q4"])
-
-        def step5():
-            arrive(c["p4"])
-            if q:
-                arrive(c["q4"])
-            start(c["all"])
-
-        def step6():
-            arrive(c["all"])
-            for group in c.values():
-                sent(group)
-
-        return [step0, step1, step2, step3, step4, step5, step6]
+            core.wait_recv()
+            for at, count, down, up, keep, last in pieces:
+                add_into(rc, at, count, lambda o, n, at=at: wg[rows(base + at + o, n), :])
+                down[0][0].start()
+
+        def reduce(step):
+            def run():
+                for at, count, down, up, keep, last in pieces:
+                    copy, own, size, spare = down[step]
+                    copy.wait_recv()
+                    add_into(rc, own, size, lambda o, n, spare=spare: inc[rows(spare + o, n), :])
+                    if step < 2:
+                        down[step + 1][0].start()
+                    else:
+                        up[2].start()
+                        keep.start()
+
+            return run
+
+        def spread(step):
+            def run():
+                for at, count, down, up, keep, last in pieces:
+                    up[step].wait_recv()
+                    if step == 2:
+                        keep.wait()
+                    if step:
+                        up[step - 1].start()
+                    else:
+                        last.start()
+
+            return run
+
+        def finish():
+            core.wait_send()
+            for at, count, down, up, keep, last in pieces:
+                last.wait_recv()
+                for copy in [d[0] for d in down] + up + [last]:
+                    copy.wait_send()
+
+        return [step0, step1, reduce(0), reduce(1), reduce(2), spread(2), spread(1), spread(0), finish]
 
     def sd_copy(k, src, dst, peer):
         return pltpu.make_async_remote_copy(
@@ -321,6 +321,10 @@
         )
 
     steps = [bucket(b) for b in range(4)] if reduce_dp else None
+
+    def now(b, s):
+        if reduce_dp:
+            steps[b][s]()
 
     def early(b, s):
         if reduce_dp:
@@ -450,11 +454,11 @@
     for j in BLOCKS:
         wg0[j, :] = dot_tn(g[:, j], dy2[...]).astype(BF16)
 
-    early(0, 0)
+    now(0, 0)
     for j in BLOCKS:
         wg1[j, :] = dot_tn(a2[:, j], dh[...]).astype(BF16)
 
-    early(1, 0)
+    now(1, 0)
     arrive(ex[DA2])
     grad_u, gain_grad, shift_grad = norm_back(summed(da2s, da2r), x2c[...], gains[1:2, :])
     grad_middle = doc[...] + grad_u
@@ -465,6 +469,7 @@
     sm[3:4, :] = shift_grad
     sm[4:5, :] = jnp.sum(grad_middle, 0, keepdims=True)
     early(0, 1)
+    early(1, 1)
     arrive(ex[DY1])
 
     att_grad = dot_nt(dy1[...], wo[...]).astype(BF16)
@@ -494,15 +499,16 @@
 
     start(ex[DA1])
     wg2[...] = dot_tn(att[...], dy1[...]).astype(BF16)
-    early(2, 0)
+    now(2, 0)
     for j in range(D // W):
         part = dot_tn(a1[:, j * W : (j + 1) * W], dqkv[...]).astype(BF16)
         for i in range(3):
             at = i * D + j * W
             wg3[at : at + W, :] = part[:, i * W : (i + 1) * W]
 
-    early(3, 0)
-    early(1, 1)
+    now(3, 0)
+    early(0, 2)
+    early(1, 2)
     arrive(ex[DA1])
     grad_u, gain_grad, shift_grad = norm_back(summed(da1s, da1r), xc[...], gains[0:1, :])
     sm[0:1, :] = gain_grad
@@ -526,54 +532,70 @@
         start(ex[OUT])
 
     if reduce_dp:
-        early(0, 2)
+        core_copy = sd_copy(0, smc.at[gc], smc.at[gc], core_peer)
+        y_copy = sd_copy(1, smy.at[gy], smy.at[gy], y_peer)
+        x_copies = [sd_copy(2 + i, smx.at[gx], smx.at[gx], x_peers[i]) for i in range(3)]
+
+    def small0():
+        arrive(ex[SMALL])
+        whole = smz[0] + smz[1] + smz[2] + smz[3]
+        own_rows = lax.broadcasted_iota(jnp.int32, (8, D), 0) >= 5
+        whole = jnp.where(own_rows, sm[...], whole)
+        if reduce_dp:
+            smc[gc] = whole
+            core_copy.start()
+        else:
+            small_out[...] = whole
+
+    def small1():
+        core_copy.wait()
+        smy[gy] = smc[0] + smc[1]
+        y_copy.start()
+
+    def small2():
+        y_copy.wait()
+        smx[gx] = smy[0] + smy[1]
+        start(x_copies)
+
+    def small3():
+        for copy in x_copies:
+            copy.wait()
+        small_out[...] = smx[0] + smx[1] + smx[2] + smx[3]
+
+    dx_copy = pltpu.make_async_copy(dxg.at[pl.ds(0, USED)], dx_out, out_sem.at[1])
+
+    def layer_results():
+        arrive(ex[OUT])
+        act_copy.start()
+        arrive(ex[DX])
+        dx_copy.start()
+
+    if reduce_dp:
         early(2, 1)
         early(3, 1)
-        early(1, 2)
-
-        @pl.when(first)
-        def _():
-            for b, s in ((0, 3), (2, 2), (3, 2), (1, 3), (0, 4), (2, 3), (3, 3), (1, 4)):
-                steps[b][s]()
 
         @pl.when(second)
         def _():
-            for s in range(5):
-                for b in range(4):
-                    if s < 4 or b < 2:
-                        steps[b][s]()
-
-        for b, s in ((0, 5), (2, 4), (3, 4), (1, 5), (2, 5), (3, 5)):
-            steps[b][s]()
-        for b in range(4):
-            steps[b][6]()
-
-    arrive(ex[OUT])
-    act_copy.start()
-    arrive(ex[DX])
-    dx_copy = pltpu.make_async_copy(dxg.at[pl.ds(0, USED)], dx_out, out_sem.at[1])
-    dx_copy.start()
-
-    arrive(ex[SMALL])
-    whole = smz[0] + smz[1] + smz[2] + smz[3]
-    own_rows = lax.broadcasted_iota(jnp.int32, (8, D), 0) >= 5
-    whole = jnp.where(own_rows, sm[...], whole)
-    if reduce_dp:
-        smc[gc] = whole
-        core_copy = sd_copy(0, smc.at[gc], smc.at[gc], core_peer)
-        core_copy.start()
-        core_copy.wait()
-        smy[gy] = smc[0] + smc[1]
-        y_copy = sd_copy(1, smy.at[gy], smy.at[gy], y_peer)
-        y_copy.start()
-        y_copy.wait()
-        smx[gx] = smy[0] + smy[1]
-        x_copies = [sd_copy(2 + i, smx.at[gx], smx.at[gx], x_peers[i]) for i in range(3)]
-        start(x_copies)
-        for copy in x_copies:
-            copy.wait()
-        whole = smx[0] + smx[1] + smx[2] + smx[3]
-    small_out[...] = whole
+            for b, s in ((0, 1), (1, 1), (0, 2), (1, 2), (2, 1), (3, 1)):
+                steps[b][s]()
+
+        def wave(*items):
+            for b, s in items:
+                steps[b][s]()
+
+        small0()
+        wave((0, 3), (1, 3), (3, 2), (2, 2))
+        small1()
+        wave((0, 4), (1, 4), (3, 3), (2, 3))
+        small2()
+        wave((0, 5), (1, 5), (3, 4), (2, 4))
+        small3()
+        layer_results()
+        wave((3, 5), (2, 5), (0, 6), (1, 6), (3, 6), (2, 6))
+        wave((0, 7), (1, 7), (3, 7), (2, 7), (0, 8), (1, 8), (3, 8), (2, 8))
+    else:
+        small0()
+        layer_results()
 
     act_copy.wait()
     dx_copy.wait()
@@ -601,7 +623,8 @@
 
 
 def call(reduce_dp, *operands):
-    hbm = pl.BlockSpec(memory_space=pl.ANY)
+    hbm = pl.BlockSpec(memory_space=pltpu.HBM)
+    anywhere = pl.BlockSpec(memory_space=pl.ANY)
     vmem = pl.BlockSpec(memory_space=pltpu.VMEM)
     smem = pl.BlockSpec(memory_space=pltpu.SMEM)
 
@@ -621,30 +644,30 @@
         low(CH, D), low(CH, D), low(CH, D), low(CH, D),
         wide(8, D), wide(4, 8, D), wide(2, 8, D), wide(2, 8, D), wide(4, 8, D),
     ]
-    scratch += [low(size, width) for size, width, p, q in BUCKETS]
-    scratch += [low(size // 2, width) for size, width, p, q in BUCKETS]
-    scratch += [low(3, p // 4, width) for size, width, p, q in BUCKETS]
-    scratch += [low(q // 2, width) for size, width, p, q in BUCKETS if q]
-    scratch += [low(p // 8, width) for size, width, p, q in BUCKETS]
-    scratch += [low(3, q // 8, width) for size, width, p, q in BUCKETS if q]
+    scratch += [low(size, width) for size, width, _ in BUCKETS]
+    scratch += [low(size // 2, width) for size, width, _ in BUCKETS]
+    scratch += [low(size * 7 // 16, width) for size, width, _ in BUCKETS]
+    scratch += [
+        pltpu.VMEM((SLOTS, ROWS), jnp.int32), wide(2, D), wide(2, D), wide(2, W), wide(2, D), wide(1, D),
+    ]
     dma = pltpu.SemaphoreType.DMA
     scratch += [
-        dma((6,)), dma((2,)), dma((11, 3)), dma((11, 3)), dma((2,)), dma((2,)),
-        dma((4, 18)), dma((4, 18)), dma((4, 2)), dma((5,)), dma((5,)),
+        dma((12,)), dma((2,)), dma((11, 3)), dma((11, 3)), dma((2,)), dma((2,)),
+        dma((4, 22)), dma((4, 22)), dma((4, 3)), dma((5,)), dma((5,)),
     ]
     return pl.pallas_call(
         functools.partial(kernel, reduce_dp),
         out_shape=[
             jax.ShapeDtypeStruct((USED, D), BF16),
             jax.ShapeDtypeStruct((USED, D), BF16),
-            *[jax.ShapeDtypeStruct((size, width), BF16) for size, width, _, _ in BUCKETS],
+            *[jax.ShapeDtypeStruct((size, width), BF16) for size, width, _ in BUCKETS],
             jax.ShapeDtypeStruct((8, D), F32),
         ],
-        in_specs=[hbm, hbm, smem, vmem, vmem, vmem, hbm, vmem, hbm, vmem, hbm, vmem, hbm],
-        out_specs=[hbm] * 6 + [vmem],
+        in_specs=[hbm, hbm, smem] + [hbm] * 10,
+        out_specs=[anywhere] * 6 + [vmem],
         scratch_shapes=scratch,
         compiler_params=pltpu.CompilerParams(
-            collective_id=0, has_side_effects=True, vmem_limit_bytes=40 * 1024 * 1024
+            collective_id=0, has_side_effects=True, vmem_limit_bytes=60 * 1024 * 1024
         ),
         name="layers",
     )(*operands)
@@ -683,7 +706,7 @@
         + [jax.ShapeDtypeStruct(shape, F32) for shape in flat],
         in_specs=[spec(a.shape) for a in lows] + [fixed((8, D))],
         out_specs=[spec(a.shape) for a in lows] + [fixed(shape) for shape in flat],
-        compiler_params=pltpu.CompilerParams(vmem_limit_bytes=40 * 1024 * 1024),
+        compiler_params=pltpu.CompilerParams(vmem_limit_bytes=60 * 1024 * 1024),
         name="widen",
     )(*lows, small)
 
@@ -708,7 +731,7 @@
         reduce_dp,
         tokens.reshape(USED, D),
         cotangent.reshape(USED, D),
-        doc_lengths.reshape(SLOTS, 3),
+        doc_lengths,
         live_mask,
         norm_gains[0],
         norm_biases[0],

time: 200 us -> 182 us (0.910)
  local copies, waits for them, and re-layouts: 11.3 us -> 0 us
  Pallas kernels: 187 us -> 181 us
    unnamed x23 -> x0, local copies, waits for them, and re-layouts: 11.3 us -> none
    pallas_call x1, Pallas kernels: 181 us -> 172 us  [call(): pl.pallas_call(functools.partial(kernel, reduce_dp), out_shape=[jax.Shape...]
    pallas_call x1, Pallas kernels: 5.91 us -> 9.5 us  [widen(): pl.pallas_call(widen_kernel, grid=(count,), out_shape=[jax.ShapeDtypeStru...]
where the time goes in v3:
time: 182 us
  Pallas kernels  181 us (99%)
    pallas_call x1, Pallas kernels, call(): pl.pallas_call(functools.partial(kernel, reduce_dp), out_shape=[jax.Shape...  172 us
    pallas_call x1, Pallas kernels, widen(): pl.pallas_call(widen_kernel, grid=(count,), out_shape=[jax.ShapeDtypeStru...  9.5 us

profile of v3, /device:TPU:1, one launch (start us, length us, event | category | flops | bytes accessed | tf_op | source)
XLA Modules:
  0.0 181.7 jit_solution(15018237767199315387)
XLA Ops:
  0.6 171.5 %layers.1 = (bf16[240,1024]{1,0:T(8,128)(2,1)}, bf16[240,1024]{1,0:T(8,128)(2,1)}, bf16[1024,1024]{1,0:T(8,128)(2,1)}, bf16[1024,1024]{1,0:T(8,128)(2,1)}, bf16[...) custom-call(f32[240,1024]{1,0:T(8,128)} %bitcast.29, f32[240,1024]{1,0:T(8,128)} %bitcast.30, ...), custom_call_target="tpu_custom_call" | custom-call | tf_op jit(solution)/shard_map/layers/pallas_call | solution.py:658
  172.2 9.5 %widen.1 = (f32[240,1024]{1,0:T(8,128)}, f32[240,1024]{1,0:T(8,128)}, f32[1024,1024]{1,0:T(8,128)}, f32[1024,1024]{1,0:T(8,128)}, f32[256,1024]{1,0:T(8,128)}, /...) custom-call(bf16[240,1024]{1,0:T(8,128)(2,1)} %get-tuple-element.29., ...), custom_call_target="tpu_custom_call" | custom-call | tf_op jit(solution)/shard_map/widen/pallas_call | solution.py:702

commit v4 on v3

--- a/solution.py
+++ b/solution.py
@@ -17,7 +17,10 @@
 USED = ROWS * SLOTS
 PAD = 256
 TEN = 4
-CH = PAD // TEN
+HALF = PAD // 2
+CH = HALF // TEN
+HALVES = (slice(0, HALF), slice(HALF, PAD))
+OWN = (slice(0, CH), slice(CH, 2 * CH))
 HEADS = 4
 HD = 64
 W = 256
@@ -68,7 +71,7 @@
     act_out, dx_out, gdn_out, gup_out, go_out, gqkv_out, small_out,
     tok, cot, wqkv, wo, wup, wdn, mask, xc, a1, qkv, prob, att, y1s, y1r, x2c, a2, slope, g,
     y2s, y2r, actg, doc, dy2, dg, dh, da2s, da2r, dx2c, dy1, dqkv, da1s, da1r, dxg,
-    pipe_f, pipe_b, pipe_fs, pipe_bs, sm, smz, smc, smy, smx,
+    pipe_f, pipe_b, pipe_fs, pipe_bs, kacc, vacc, sm, smz, smc, smy, smx,
     wg0, wg1, wg2, wg3, rc0, rc1, rc2, rc3, in0, in1, in2, in3,
     live, gains, shifts, qvb, obias, upb,
     load_sem, out_sem, tp_s, tp_r, pp_s, pp_r, dp_s, dp_r, dp_l, sd_s, sd_r,
@@ -85,7 +88,7 @@
     core_peer = gx * 4 + gy * 2 + (1 - gc)
     y_peer = gx * 4 + (1 - gy) * 2 + gc
     x_peers = [((gx + t) % 4) * 4 + gy * 2 + gc for t in (1, 2, 3)]
-    mine = tile(z, CH)
+    mine = [pl.ds(pl.multiple_of(h * HALF + z * CH, CH), CH) for h in range(2)]
     cube_bits = (((gx + 1) // 2) % 2, gx // 2, gy)
     cube_peers = (
         (gx + 1 - 2 * (gx % 2)) * 4 + gy * 2 + gc,
@@ -160,21 +163,25 @@
 
     pl.semaphore_wait(barrier, len(partners))
 
-    def tp_copy(k, t, src, dst):
+    def tp_copy(k, h, t, src, dst):
         return pltpu.make_async_remote_copy(
             src_ref=src,
             dst_ref=dst,
-            send_sem=tp_s.at[k, t - 1],
-            recv_sem=tp_r.at[k, t - 1],
+            send_sem=tp_s.at[2 * k + h, t - 1],
+            recv_sem=tp_r.at[2 * k + h, t - 1],
             device_id={"tensor": (z + t) % 4},
             device_id_type=MESH,
         )
 
-    def scatter(k, src, dst):
-        return [tp_copy(k, t, src.at[tile((z + t) % 4, CH)], dst.at[t - 1]) for t in (2, 1, 3)]
-
-    def gather(k, buf):
-        return [tp_copy(k, t, buf.at[mine], buf.at[mine]) for t in (2, 1, 3)]
+    def scatter(k, h, src, dst):
+        copies = []
+        for t in (2, 1, 3):
+            at = pl.multiple_of(h * HALF + ((z + t) % 4) * CH, CH)
+            copies.append(tp_copy(k, h, t, src.at[pl.ds(at, CH)], dst.at[h, t - 1]))
+        return copies
+
+    def gather(k, h, buf):
+        return [tp_copy(k, h, t, buf.at[mine[h]], buf.at[mine[h]]) for t in (2, 1, 3)]
 
     def start(copies):
         for copy in copies:
@@ -188,32 +195,30 @@
         for copy in copies:
             copy.wait_send()
 
-    ex = {
-        A1: gather(A1, a1),
-        Y1: scatter(Y1, y1s, y1r),
-        A2: gather(A2, a2),
-        Y2: scatter(Y2, y2s, y2r),
-        OUT: gather(OUT, actg),
-        DOUT: gather(DOUT, dy2),
-        DA2: scatter(DA2, da2s, da2r),
-        DY1: gather(DY1, dy1),
-        DA1: scatter(DA1, da1s, da1r),
-        DX: gather(DX, dxg),
-        SMALL: [tp_copy(SMALL, t, smz.at[z], smz.at[z]) for t in (2, 1, 3)],
-    }
-    forth = pltpu.make_async_remote_copy(
-        src_ref=pipe_fs, dst_ref=pipe_f, send_sem=pp_s.at[0], recv_sem=pp_r.at[0],
-        device_id={"pipe": 1 - pipe}, device_id_type=MESH,
-    )
-    back = pltpu.make_async_remote_copy(
-        src_ref=pipe_bs, dst_ref=pipe_b, send_sem=pp_s.at[1], recv_sem=pp_r.at[1],
-        device_id={"pipe": 1 - pipe}, device_id_type=MESH,
-    )
-
-    def summed(src, dst):
-        total = src[mine].astype(F32)
+    ex = {}
+    for h in range(2):
+        for k, buf in ((A1, a1), (A2, a2), (OUT, actg), (DOUT, dy2), (DY1, dy1), (DX, dxg)):
+            ex[k, h] = gather(k, h, buf)
+        for k, src, dst in ((Y1, y1s, y1r), (Y2, y2s, y2r), (DA2, da2s, da2r), (DA1, da1s, da1r)):
+            ex[k, h] = scatter(k, h, src, dst)
+    ex[SMALL, 0] = [tp_copy(SMALL, 0, t, smz.at[z], smz.at[z]) for t in (2, 1, 3)]
+
+    def hand_over(src, dst, k):
+        return [
+            pltpu.make_async_remote_copy(
+                src_ref=src.at[h], dst_ref=dst.at[h], send_sem=pp_s.at[k + h], recv_sem=pp_r.at[k + h],
+                device_id={"pipe": 1 - pipe}, device_id_type=MESH,
+            )
+            for h in range(2)
+        ]
+
+    forth = hand_over(pipe_fs, pipe_f, 0)
+    back = hand_over(pipe_bs, pipe_b, 2)
+
+    def summed(src, dst, h):
+        total = src[mine[h], :].astype(F32)
         for t in range(3):
-            total = total + dst[t].astype(F32)
+            total = total + dst[h, t].astype(F32)
         return total
 
     def dp_copy(b, k, src, dst, peer):
@@ -330,21 +335,15 @@
         if reduce_dp:
             pl.when(first)(steps[b][s])
 
+    def output_grads(h):
+        half = HALVES[h]
+        for j in BLOCKS:
+            dg[half, j] = dot_nt(dy2[half, :], wdn[j, :])
+
     @pl.when(first)
     def _():
         loads["tok"].wait()
         tok[pl.ds(USED, PAD - USED), :] = jnp.zeros((PAD - USED, D), F32)
-
-        @pl.loop(0, TEN)
-        def _(i):
-            unit, _ = normed(tok[tile(i, CH), :])
-            a1[tile(i, CH), :] = (unit * gains[0:1, :] + shifts[0:1, :]).astype(BF16)
-
-        xc[...] = tok[mine, :]
-
-    def output_grads():
-        for j in BLOCKS:
-            dg[:, j] = dot_nt(dy2[...], wdn[j, :])
 
     @pl.when(second)
     def _():
@@ -354,182 +353,257 @@
         cot[...] = masked
         dy2[...] = masked.astype(BF16)
         sm[5:6, :] = jnp.sum(masked, 0, keepdims=True)
-        doc[...] = cot[mine, :]
         loads["dn"].wait()
-        output_grads()
-        forth.wait_recv()
-        inputs = pipe_f[...].astype(F32)
-        xc[...] = inputs
-        unit, _ = normed(inputs)
-        a1[mine, :] = (unit * gains[0:1, :] + shifts[0:1, :]).astype(BF16)
-        start(ex[A1])
-        arrive(ex[A1])
-
+        for h in range(2):
+            doc[OWN[h], :] = cot[mine[h], :]
+            output_grads(h)
+
+    def take(h):
+        half = HALVES[h]
+
+        @pl.when(first)
+        def _():
+            unit, _ = normed(tok[half, :])
+            a1[half, :] = (unit * gains[0:1, :] + shifts[0:1, :]).astype(BF16)
+            xc[OWN[h], :] = tok[mine[h], :]
+
+        @pl.when(second)
+        def _():
+            forth[h].wait_recv()
+            inputs = pipe_f[h].astype(F32)
+            xc[OWN[h], :] = inputs
+            unit, _ = normed(inputs)
+            a1[mine[h], :] = (unit * gains[0:1, :] + shifts[0:1, :]).astype(BF16)
+            start(ex[A1, h])
+            arrive(ex[A1, h])
+
+    def head_rows(values, n):
+        return (values.astype(F32) * jnp.where(head_of == n, 1.0, 0.0)).astype(BF16)
+
+    def attend(h):
+        half, keys = HALVES[h], slice(0, (h + 1) * HALF)
+        for j in range(3):
+            part = dot_nn(a1[half, :], wqkv[j])
+            if j != 1:
+                part = part + qvb[j // 2 : j // 2 + 1, :]
+            qkv[half, j * W : (j + 1) * W] = part.astype(BF16)
+        attended = jnp.zeros((HALF, W), F32)
+        for n in range(HEADS):
+            scores = dot_nt(head_rows(qkv[half, 0:W], n), qkv[keys, W : 2 * W]) * (1.0 / math.sqrt(HD))
+            scores = jnp.where(mask[half, keys] > 0.5, scores, -1000000000.0)
+            expo = jnp.exp(scores - jnp.max(scores, -1, keepdims=True))
+            p = expo / jnp.sum(expo, -1, keepdims=True)
+            prob[n, half, keys] = p
+            attended = attended + dot_nn(p.astype(BF16), head_rows(qkv[keys, 2 * W : 3 * W], n))
+        att[half, :] = attended.astype(BF16)
+        if h == 0:
+            loads["o"].wait()
+        for j in BLOCKS:
+            y1s[half, j] = dot_nn(att[half, :], wo[:, j]).astype(BF16)
+        start(ex[Y1, h])
+
+    def middle(h):
+        arrive(ex[Y1, h])
+        value = xc[OWN[h], :] + summed(y1s, y1r, h) + obias[0:1, :]
+        x2c[OWN[h], :] = value
+        unit, _ = normed(value)
+        a2[mine[h], :] = (unit * gains[1:2, :] + shifts[1:2, :]).astype(BF16)
+        start(ex[A2, h])
+
+    def feed(h):
+        half = HALVES[h]
+        arrive(ex[A2, h])
+        for j in BLOCKS:
+            hidden = dot_nn(a2[half, :], wup[:, j]) + upb[:, j]
+            square = hidden * hidden
+            root = math.sqrt(2.0 / math.pi)
+            bent = jnp.tanh(root * hidden * (1.0 + 0.044715 * square))
+            lifted = 0.5 * (1.0 + bent)
+            g[half, j] = (hidden * lifted).astype(BF16)
+            inner = root * (1.0 + 3.0 * 0.044715 * square)
+            slope[half, j] = lifted + 0.5 * hidden * (1.0 - bent * bent) * inner
+
+    def down(h):
+        half = HALVES[h]
+        for j in BLOCKS:
+            y2s[half, j] = dot_nn(g[half, :], wdn[:, j]).astype(BF16)
+        start(ex[Y2, h])
+
+    def layer_output(h):
+        arrive(ex[Y2, h])
+        result = (x2c[OWN[h], :] + summed(y2s, y2r, h) + obias[1:2, :]).astype(BF16)
+        pipe_fs[h] = result
+        actg[mine[h], :] = result
+
+    take(0)
     loads["qkv"].wait()
-    for j in range(3):
-        part = dot_nn(a1[...], wqkv[j])
-        if j != 1:
-            part = part + qvb[j // 2 : j // 2 + 1, :]
-        qkv[:, j * W : (j + 1) * W] = part.astype(BF16)
-
-    def head_rows(values, h):
-        return (values.astype(F32) * jnp.where(head_of == h, 1.0, 0.0)).astype(BF16)
-
-    attended = jnp.zeros((PAD, W), F32)
-    for h in range(HEADS):
-        scores = dot_nt(head_rows(qkv[:, 0:W], h), qkv[:, W : 2 * W]) * (1.0 / math.sqrt(HD))
-        scores = jnp.where(mask[...] > 0.5, scores, -1000000000.0)
-        expo = jnp.exp(scores - jnp.max(scores, -1, keepdims=True))
-        p = expo / jnp.sum(expo, -1, keepdims=True)
-        prob[h] = p
-        attended = attended + dot_nn(p.astype(BF16), head_rows(qkv[:, 2 * W : 3 * W], h))
-
-    att[...] = attended.astype(BF16)
-    loads["o"].wait()
-    for j in BLOCKS:
-        y1s[:, j] = dot_nn(att[...], wo[:, j]).astype(BF16)
-
-    start(ex[Y1])
-    arrive(ex[Y1])
-    middle = xc[...] + summed(y1s, y1r) + obias[0:1, :]
-    x2c[...] = middle
-    unit, _ = normed(middle)
-    a2[mine, :] = (unit * gains[1:2, :] + shifts[1:2, :]).astype(BF16)
-    start(ex[A2])
+    attend(0)
+    take(1)
+    attend(1)
+    middle(0)
+    middle(1)
     loads["up"].wait()
-    arrive(ex[A2])
-
-    for j in BLOCKS:
-        hidden = dot_nn(a2[...], wup[:, j]) + upb[:, j]
-        square = hidden * hidden
-        root = math.sqrt(2.0 / math.pi)
-        bent = jnp.tanh(root * hidden * (1.0 + 0.044715 * square))
-        lifted = 0.5 * (1.0 + bent)
-        g[:, j] = (hidden * lifted).astype(BF16)
-        inner = root * (1.0 + 3.0 * 0.044715 * square)
-        slope[:, j] = lifted + 0.5 * hidden * (1.0 - bent * bent) * inner
-
-    def down():
+
+    @pl.when(first)
+    def _():
+        loads["dn"].wait()
+
+    for h in range(2):
+        feed(h)
+        pl.when(first)(functools.partial(down, h))
+
+    act_copy = pltpu.make_async_copy(actg.at[pl.ds(0, USED)], act_out, out_sem.at[0])
+
+    def feed_back(h):
+        half = HALVES[h]
         for j in BLOCKS:
-            y2s[:, j] = dot_nn(g[...], wdn[:, j]).astype(BF16)
-
-        start(ex[Y2])
-
-    def layer_output():
-        arrive(ex[Y2])
-        result = (x2c[...] + summed(y2s, y2r) + obias[1:2, :]).astype(BF16)
-        pipe_fs[...] = result
-        actg[mine, :] = result
-
-    act_copy = pltpu.make_async_copy(actg.at[pl.ds(0, USED)], act_out, out_sem.at[0])
+            grad = (dg[half, j] * slope[half, j]).astype(BF16)
+            dh[half, j] = grad
+            sm[7:8, j] += jnp.sum(grad.astype(F32), 0, keepdims=True)
+        for j in BLOCKS:
+            da2s[half, j] = dot_nt(dh[half, :], wup[j, :]).astype(BF16)
+        start(ex[DA2, h])
+
+    def receive(h):
+        back[h].wait_recv()
+        dy2[mine[h], :] = pipe_b[h]
+        doc[OWN[h], :] = pipe_b[h].astype(F32)
+        start(ex[DOUT, h])
 
     @pl.when(first)
     def _():
-        loads["dn"].wait()
-        down()
-        layer_output()
-        forth.start()
-        start(ex[OUT])
-        back.wait_recv()
-        dy2[mine, :] = pipe_b[...]
-        doc[...] = pipe_b[...].astype(F32)
-        start(ex[DOUT])
-        arrive(ex[DOUT])
-        output_grads()
-
-    for j in BLOCKS:
-        grad = (dg[:, j] * slope[:, j]).astype(BF16)
-        dh[:, j] = grad
-        sm[7:8, j] = jnp.sum(grad.astype(F32), 0, keepdims=True)
-
-    for j in BLOCKS:
-        da2s[:, j] = dot_nt(dh[...], wup[j, :]).astype(BF16)
-
-    start(ex[DA2])
+        for h in range(2):
+            layer_output(h)
+            forth[h].start()
+            start(ex[OUT, h])
+        receive(1)
+        arrive(ex[DOUT, 1])
+        receive(0)
+        output_grads(1)
+
+    feed_back(1)
 
     @pl.when(first)
     def _():
-        sm[5:6, :] = jnp.sum(dy2[...].astype(F32), 0, keepdims=True)
-
-    for j in BLOCKS:
-        wg0[j, :] = dot_tn(g[:, j], dy2[...]).astype(BF16)
-
-    now(0, 0)
-    for j in BLOCKS:
-        wg1[j, :] = dot_tn(a2[:, j], dh[...]).astype(BF16)
-
-    now(1, 0)
-    arrive(ex[DA2])
-    grad_u, gain_grad, shift_grad = norm_back(summed(da2s, da2r), x2c[...], gains[1:2, :])
-    grad_middle = doc[...] + grad_u
-    dy1[mine, :] = grad_middle.astype(BF16)
-    start(ex[DY1])
-    dx2c[...] = grad_middle
-    sm[1:2, :] = gain_grad
-    sm[3:4, :] = shift_grad
-    sm[4:5, :] = jnp.sum(grad_middle, 0, keepdims=True)
+        arrive(ex[DOUT, 0])
+        output_grads(0)
+
+    feed_back(0)
+
+    def down_grad():
+        for j in BLOCKS:
+            wg0[j, :] = dot_tn(g[:, j], dy2[...]).astype(BF16)
+        now(0, 0)
+
+    def up_grad():
+        for j in BLOCKS:
+            wg1[j, :] = dot_tn(a2[:, j], dh[...]).astype(BF16)
+        now(1, 0)
+
+    def attention_grads():
+        wg2[...] = dot_tn(att[...], dy1[...]).astype(BF16)
+        now(2, 0)
+        for j in range(D // W):
+            part = dot_tn(a1[:, j * W : (j + 1) * W], dqkv[...]).astype(BF16)
+            for i in range(3):
+                at = i * D + j * W
+                wg3[at : at + W, :] = part[:, i * W : (i + 1) * W]
+        now(3, 0)
+
+    def middle_back(h):
+        arrive(ex[DA2, h])
+        grad_u, gain_grad, shift_grad = norm_back(
+            summed(da2s, da2r, h), x2c[OWN[h], :], gains[1:2, :]
+        )
+        grad_middle = doc[OWN[h], :] + grad_u
+        dy1[mine[h], :] = grad_middle.astype(BF16)
+        start(ex[DY1, h])
+        dx2c[OWN[h], :] = grad_middle
+        sm[1:2, :] += gain_grad
+        sm[3:4, :] += shift_grad
+        sm[4:5, :] += jnp.sum(grad_middle, 0, keepdims=True)
+
+    pl.when(first)(down_grad)
+    middle_back(1)
+    pl.when(first)(up_grad)
+    middle_back(0)
     early(0, 1)
     early(1, 1)
-    arrive(ex[DY1])
-
-    att_grad = dot_nt(dy1[...], wo[...]).astype(BF16)
-    dqkv[:, 2 * W : 3 * W] = att_grad
-    grad_q = grad_k = grad_v = jnp.zeros((PAD, W), F32)
-    for h in range(HEADS):
-        p = prob[h]
-        own = head_rows(dqkv[:, 2 * W : 3 * W], h)
-        grad_p = dot_nt(own, qkv[:, 2 * W : 3 * W])
-        grad_v = grad_v + dot_tn(p.astype(BF16), own)
-        grad_s = p * (grad_p - jnp.sum(grad_p * p, -1, keepdims=True))
-        grad_s = grad_s.astype(BF16)
-        grad_q = grad_q + dot_nn(grad_s, head_rows(qkv[:, W : 2 * W], h))
-        grad_k = grad_k + dot_tn(grad_s, head_rows(qkv[:, 0:W], h))
-
-    scale = 1.0 / math.sqrt(HD)
-    for j, (grad, factor) in enumerate(((grad_q, scale), (grad_k, scale), (grad_v, 1.0))):
-        low = (grad * factor).astype(BF16)
-        dqkv[:, j * W : (j + 1) * W] = low
-        if j != 1:
-            at = (j // 2) * W
-            sm[6:7, at : at + W] = jnp.sum(low.astype(F32), 0, keepdims=True)
-
-    for j in BLOCKS:
-        part = dot_nt(dqkv[:, 0:W], wqkv[0, j, :]) + dot_nt(dqkv[:, W : 2 * W], wqkv[1, j, :])
-        da1s[:, j] = (part + dot_nt(dqkv[:, 2 * W : 3 * W], wqkv[2, j, :])).astype(BF16)
-
-    start(ex[DA1])
-    wg2[...] = dot_tn(att[...], dy1[...]).astype(BF16)
-    now(2, 0)
-    for j in range(D // W):
-        part = dot_tn(a1[:, j * W : (j + 1) * W], dqkv[...]).astype(BF16)
-        for i in range(3):
-            at = i * D + j * W
-            wg3[at : at + W, :] = part[:, i * W : (i + 1) * W]
-
-    now(3, 0)
+
+    def attend_back(h):
+        half, keys = HALVES[h], slice(0, (h + 1) * HALF)
+        count = (h + 1) * HALF
+        arrive(ex[DY1, h])
+        dqkv[half, 2 * W : 3 * W] = dot_nt(dy1[half, :], wo[...]).astype(BF16)
+        grad_q = jnp.zeros((HALF, W), F32)
+        grad_k = grad_v = jnp.zeros((count, W), F32)
+        for n in range(HEADS):
+            p = prob[n, half, keys]
+            own = head_rows(dqkv[half, 2 * W : 3 * W], n)
+            grad_p = dot_nt(own, qkv[keys, 2 * W : 3 * W])
+            grad_v = grad_v + dot_tn(p.astype(BF16), own)
+            grad_s = p * (grad_p - jnp.sum(grad_p * p, -1, keepdims=True))
+            grad_s = grad_s.astype(BF16)
+            grad_q = grad_q + dot_nn(grad_s, head_rows(qkv[keys, W : 2 * W], n))
+            grad_k = grad_k + dot_tn(grad_s, head_rows(qkv[half, 0:W], n))
+        if h:
+            kacc[...] = grad_k[0:HALF]
+            vacc[...] = grad_v[0:HALF]
+            grad_k, grad_v = grad_k[HALF:], grad_v[HALF:]
+        else:
+            grad_k, grad_v = grad_k + kacc[...], grad_v + vacc[...]
+        scale = 1.0 / math.sqrt(HD)
+        for j, (grad, factor) in enumerate(((grad_q, scale), (grad_k, scale), (grad_v, 1.0))):
+            low = (grad * factor).astype(BF16)
+            dqkv[half, j * W : (j + 1) * W] = low
+            if j != 1:
+                at = (j // 2) * W
+                sm[6:7, at : at + W] += jnp.sum(low.astype(F32), 0, keepdims=True)
+        for j in BLOCKS:
+            part = dot_nt(dqkv[half, 0:W], wqkv[0, j, :])
+            part = part + dot_nt(dqkv[half, W : 2 * W], wqkv[1, j, :])
+            part = part + dot_nt(dqkv[half, 2 * W : 3 * W], wqkv[2, j, :])
+            da1s[half, j] = part.astype(BF16)
+        start(ex[DA1, h])
+
+    def input_grads(h):
+        arrive(ex[DA1, h])
+        grad_u, gain_grad, shift_grad = norm_back(
+            summed(da1s, da1r, h), xc[OWN[h], :], gains[0:1, :]
+        )
+        low = (dx2c[OWN[h], :] + grad_u).astype(BF16)
+        pipe_bs[h] = low
+        pl.when(second)(lambda: back[h].start())
+        dxg[mine[h], :] = low
+        start(ex[DX, h])
+        sm[0:1, :] += gain_grad
+        sm[2:3, :] += shift_grad
+
+    attend_back(1)
+    attend_back(0)
     early(0, 2)
+    pl.when(first)(attention_grads)
     early(1, 2)
-    arrive(ex[DA1])
-    grad_u, gain_grad, shift_grad = norm_back(summed(da1s, da1r), xc[...], gains[0:1, :])
-    sm[0:1, :] = gain_grad
-    sm[2:3, :] = shift_grad
-    low = (dx2c[...] + grad_u).astype(BF16)
-    pipe_bs[...] = low
-    dxg[mine, :] = low
+    input_grads(1)
+    input_grads(0)
+
+    @pl.when(first)
+    def _():
+        sm[5:6, :] = jnp.sum(dy2[...].astype(F32), 0, keepdims=True)
+
+    smz[z] = sm[...]
+    start(ex[SMALL, 0])
 
     @pl.when(second)
     def _():
-        back.start()
-
-    start(ex[DX])
-    smz[z] = sm[...]
-    start(ex[SMALL])
-
-    @pl.when(second)
-    def _():
-        down()
-        layer_output()
-        start(ex[OUT])
+        for h in range(2):
+            down(h)
+        down_grad()
+        up_grad()
+        attention_grads()
+        for h in range(2):
+            layer_output(h)
+            start(ex[OUT, h])
 
     if reduce_dp:
         core_copy = sd_copy(0, smc.at[gc], smc.at[gc], core_peer)
@@ -537,7 +611,7 @@
         x_copies = [sd_copy(2 + i, smx.at[gx], smx.at[gx], x_peers[i]) for i in range(3)]
 
     def small0():
-        arrive(ex[SMALL])
+        arrive(ex[SMALL, 0])
         whole = smz[0] + smz[1] + smz[2] + smz[3]
         own_rows = lax.broadcasted_iota(jnp.int32, (8, D), 0) >= 5
         whole = jnp.where(own_rows, sm[...], whole)
@@ -565,9 +639,10 @@
     dx_copy = pltpu.make_async_copy(dxg.at[pl.ds(0, USED)], dx_out, out_sem.at[1])
 
     def layer_results():
-        arrive(ex[OUT])
+        for h in range(2):
+            arrive(ex[OUT, h])
+            arrive(ex[DX, h])
         act_copy.start()
-        arrive(ex[DX])
         dx_copy.start()
 
     if reduce_dp:
@@ -599,18 +674,22 @@
 
     act_copy.wait()
     dx_copy.wait()
-    for k in (Y1, A2, Y2, OUT, DA2, DY1, DA1, DX, SMALL):
-        sent(ex[k])
+    sent(ex[SMALL, 0])
+    for h in range(2):
+        for k in (Y1, A2, Y2, OUT, DA2, DY1, DA1, DX):
+            sent(ex[k, h])
 
     @pl.when(first)
     def _():
-        forth.wait_send()
-        sent(ex[DOUT])
+        for h in range(2):
+            forth[h].wait_send()
+            sent(ex[DOUT, h])
 
     @pl.when(second)
     def _():
-        back.wait_send()
-        sent(ex[A1])
+        for h in range(2):
+            back[h].wait_send()
+            sent(ex[A1, h])
 
     if not reduce_dp:
         copies = [
@@ -636,12 +715,12 @@
 
     scratch = [
         wide(PAD, D), wide(PAD, D), low(3, D, W), low(256, D), low(D, D), low(D, D),
-        wide(PAD, PAD), wide(CH, D), low(PAD, D), low(PAD, 768), wide(HEADS, PAD, PAD), low(PAD, W),
-        low(PAD, D), low(3, CH, D), wide(CH, D), low(PAD, D), wide(PAD, D), low(PAD, D),
-        low(PAD, D), low(3, CH, D), low(PAD, D), wide(CH, D), low(PAD, D), wide(PAD, D), low(PAD, D),
-        low(PAD, D), low(3, CH, D), wide(CH, D), low(PAD, D), low(PAD, 768), low(PAD, D),
-        low(3, CH, D), low(PAD, D),
-        low(CH, D), low(CH, D), low(CH, D), low(CH, D),
+        wide(PAD, PAD), wide(2 * CH, D), low(PAD, D), low(PAD, 768), wide(HEADS, PAD, PAD), low(PAD, W),
+        low(PAD, D), low(2, 3, CH, D), wide(2 * CH, D), low(PAD, D), wide(PAD, D), low(PAD, D),
+        low(PAD, D), low(2, 3, CH, D), low(PAD, D), wide(2 * CH, D), low(PAD, D), wide(PAD, D), low(PAD, D),
+        low(PAD, D), low(2, 3, CH, D), wide(2 * CH, D), low(PAD, D), low(PAD, 768), low(PAD, D),
+        low(2, 3, CH, D), low(PAD, D),
+        low(2, CH, D), low(2, CH, D), low(2, CH, D), low(2, CH, D), wide(HALF, W), wide(HALF, W),
         wide(8, D), wide(4, 8, D), wide(2, 8, D), wide(2, 8, D), wide(4, 8, D),
     ]
     scratch += [low(size, width) for size, width, _ in BUCKETS]
@@ -652,7 +731,7 @@
     ]
     dma = pltpu.SemaphoreType.DMA
     scratch += [
-        dma((12,)), dma((2,)), dma((11, 3)), dma((11, 3)), dma((2,)), dma((2,)),
+        dma((12,)), dma((2,)), dma((22, 3)), dma((22, 3)), dma((4,)), dma((4,)),
         dma((4, 22)), dma((4, 22)), dma((4, 3)), dma((5,)), dma((5,)),
     ]
     return pl.pallas_call(

time: 182 us -> 165 us (0.907)
  Pallas kernels: 181 us -> 164 us
    pallas_call x1, Pallas kernels: 172 us -> 155 us  [call(): pl.pallas_call(functools.partial(kernel, reduce_dp), out_shape=[jax.Shape...]
where the time goes in v4:
time: 165 us
  Pallas kernels  164 us (99%)
    pallas_call x1, Pallas kernels, call(): pl.pallas_call(functools.partial(kernel, reduce_dp), out_shape=[jax.Shape...  155 us
    pallas_call x1, Pallas kernels, widen(): pl.pallas_call(widen_kernel, grid=(count,), out_shape=[jax.ShapeDtypeStru...  9.5 us

profile of v4, /device:TPU:1, one launch (start us, length us, event | category | flops | bytes accessed | tf_op | source)
XLA Modules:
  0.0 165.0 jit_solution(661583701648791066)
XLA Ops:
  0.6 154.7 %layers.1 = (bf16[240,1024]{1,0:T(8,128)(2,1)}, bf16[240,1024]{1,0:T(8,128)(2,1)}, bf16[1024,1024]{1,0:T(8,128)(2,1)}, bf16[1024,1024]{1,0:T(8,128)(2,1)}, bf16[...) custom-call(f32[240,1024]{1,0:T(8,128)} %bitcast.29, f32[240,1024]{1,0:T(8,128)} %bitcast.30, ...), custom_call_target="tpu_custom_call" | custom-call | tf_op jit(solution)/shard_map/layers/pallas_call | solution.py:737
  155.3 9.5 %widen.1 = (f32[240,1024]{1,0:T(8,128)}, f32[240,1024]{1,0:T(8,128)}, f32[1024,1024]{1,0:T(8,128)}, f32[1024,1024]{1,0:T(8,128)}, f32[256,1024]{1,0:T(8,128)}, /...) custom-call(bf16[240,1024]{1,0:T(8,128)(2,1)} %get-tuple-element.29., ...), custom_call_target="tpu_custom_call" | custom-call | tf_op jit(solution)/shard_map/widen/pallas_call | solution.py:781

commit v5 on v4

--- a/solution.py
+++ b/solution.py
@@ -29,9 +29,11 @@
     (1024, 1024, (256, 128, 128)),
     (1024, 1024, (128, 256, 128)),
     (256, 1024, (0, 0, 128)),
-    (3072, 256, (512, 512, 512)),
+    (1536, 256, (256, 256, 256)),
+    (1536, 256, (256, 256, 256)),
 )
-A1, Y1, A2, Y2, OUT, DOUT, DA2, DY1, DA1, DX, SMALL = range(11)
+PLACE = (0, 0, 0, 0, 1536)
+Y1, A2, Y2, OUT, DA2, DY1, DA1, DX, SMALL = range(9)
 
 
 def dot_nn(a, b):
@@ -71,14 +73,14 @@
     act_out, dx_out, gdn_out, gup_out, go_out, gqkv_out, small_out,
     tok, cot, wqkv, wo, wup, wdn, mask, xc, a1, qkv, prob, att, y1s, y1r, x2c, a2, slope, g,
     y2s, y2r, actg, doc, dy2, dg, dh, da2s, da2r, dx2c, dy1, dqkv, da1s, da1r, dxg,
-    pipe_f, pipe_b, pipe_fs, pipe_bs, kacc, vacc, sm, smz, smc, smy, smx,
-    wg0, wg1, wg2, wg3, rc0, rc1, rc2, rc3, in0, in1, in2, in3,
+    pipe_f, pipe_fs, pipe_bs, kacc, vacc, sm, smz, smc, smy, smx,
+    wg0, wg1, wg2, wg3, wg4, rc0, rc1, rc2, rc3, rc4, in0, in1, in2, in3, in4,
     live, gains, shifts, qvb, obias, upb,
     load_sem, out_sem, tp_s, tp_r, pp_s, pp_r, dp_s, dp_r, dp_l, sd_s, sd_r,
 ):
-    wgs, rcs = (wg0, wg1, wg2, wg3), (rc0, rc1, rc2, rc3)
-    ins = (in0, in1, in2, in3)
-    gouts = (gdn_out, gup_out, go_out, gqkv_out)
+    wgs, rcs = (wg0, wg1, wg2, wg3, wg4), (rc0, rc1, rc2, rc3, rc4)
+    ins = (in0, in1, in2, in3, in4)
+    gouts = (gdn_out, gup_out, go_out, gqkv_out, gqkv_out)
     pipe = lax.axis_index("pipe")
     dp = lax.axis_index("dp")
     z = lax.axis_index("tensor")
@@ -129,7 +131,8 @@
             loads[name].start()
 
     barrier = pltpu.get_barrier_semaphore()
-    partners = [{"tensor": (z + t) % 4} for t in (1, 2, 3)] + [{"pipe": 1 - pipe}]
+    partners = [{"tensor": (z + t) % 4} for t in (1, 2, 3)]
+    partners += [{"pipe": 1 - pipe, "tensor": (z + t) % 4} for t in range(4)]
     if reduce_dp:
         partners += [{"dp": core_peer}, {"dp": y_peer}] + [{"dp": p} for p in x_peers]
     for partner in partners:
@@ -161,8 +164,6 @@
     sm[...] = jnp.zeros_like(sm)
     head_of = lax.broadcasted_iota(jnp.int32, (1, W), 1) // HD
 
-    pl.semaphore_wait(barrier, len(partners))
-
     def tp_copy(k, h, t, src, dst):
         return pltpu.make_async_remote_copy(
             src_ref=src,
@@ -197,23 +198,24 @@
 
     ex = {}
     for h in range(2):
-        for k, buf in ((A1, a1), (A2, a2), (OUT, actg), (DOUT, dy2), (DY1, dy1), (DX, dxg)):
+        for k, buf in ((A2, a2), (OUT, actg), (DY1, dy1), (DX, dxg)):
             ex[k, h] = gather(k, h, buf)
         for k, src, dst in ((Y1, y1s, y1r), (Y2, y2s, y2r), (DA2, da2s, da2r), (DA1, da1s, da1r)):
             ex[k, h] = scatter(k, h, src, dst)
     ex[SMALL, 0] = [tp_copy(SMALL, 0, t, smz.at[z], smz.at[z]) for t in (2, 1, 3)]
 
-    def hand_over(src, dst, k):
+    def hand_over(src, dst, k, h):
         return [
             pltpu.make_async_remote_copy(
-                src_ref=src.at[h], dst_ref=dst.at[h], send_sem=pp_s.at[k + h], recv_sem=pp_r.at[k + h],
-                device_id={"pipe": 1 - pipe}, device_id_type=MESH,
+                src_ref=src.at[h], dst_ref=dst.at[mine[h]],
+                send_sem=pp_s.at[k + h, t], recv_sem=pp_r.at[k + h, t],
+                device_id={"pipe": 1 - pipe, "tensor": (z + t) % 4}, device_id_type=MESH,
             )
-            for h in range(2)
+            for t in (2, 1, 3, 0)
         ]
 
-    forth = hand_over(pipe_fs, pipe_f, 0)
-    back = hand_over(pipe_bs, pipe_b, 2)
+    forth = [hand_over(pipe_fs, pipe_f, 0, h) for h in range(2)]
+    back = [hand_over(pipe_bs, dy2, 2, h) for h in range(2)]
 
     def summed(src, dst, h):
         total = src[mine[h], :].astype(F32)
@@ -243,7 +245,7 @@
         size, _, parts = BUCKETS[b]
         half = size // 2
         wg, rc, inc, out = wgs[b], rcs[b], ins[b], gouts[b]
-        base = gc * half
+        base = PLACE[b] + gc * half
         whole = rows((1 - gc) * half, half)
         core = dp_copy(b, 0, wg.at[whole], rc, core_peer)
         pieces = []
@@ -280,7 +282,7 @@
         def step1():
             core.wait_recv()
             for at, count, down, up, keep, last in pieces:
-                add_into(rc, at, count, lambda o, n, at=at: wg[rows(base + at + o, n), :])
+                add_into(rc, at, count, lambda o, n, at=at: wg[rows(gc * half + at + o, n), :])
                 down[0][0].start()
 
         def reduce(step):
@@ -325,7 +327,7 @@
             device_id={"dp": peer}, device_id_type=MESH,
         )
 
-    steps = [bucket(b) for b in range(4)] if reduce_dp else None
+    steps = [bucket(b) for b in range(5)] if reduce_dp else None
 
     def now(b, s):
         if reduce_dp:
@@ -369,13 +371,10 @@
 
         @pl.when(second)
         def _():
-            forth[h].wait_recv()
-            inputs = pipe_f[h].astype(F32)
-            xc[OWN[h], :] = inputs
-            unit, _ = normed(inputs)
-            a1[mine[h], :] = (unit * gains[0:1, :] + shifts[0:1, :]).astype(BF16)
-            start(ex[A1, h])
-            arrive(ex[A1, h])
+            arrive(forth[h])
+            unit, _ = normed(pipe_f[half, :].astype(F32))
+            a1[half, :] = (unit * gains[0:1, :] + shifts[0:1, :]).astype(BF16)
+            xc[OWN[h], :] = pipe_f[mine[h], :].astype(F32)
 
     def head_rows(values, n):
         return (values.astype(F32) * jnp.where(head_of == n, 1.0, 0.0)).astype(BF16)
@@ -400,6 +399,8 @@
             loads["o"].wait()
         for j in BLOCKS:
             y1s[half, j] = dot_nn(att[half, :], wo[:, j]).astype(BF16)
+        if h == 0:
+            pl.semaphore_wait(barrier, len(partners))
         start(ex[Y1, h])
 
     def middle(h):
@@ -454,6 +455,26 @@
 
     act_copy = pltpu.make_async_copy(actg.at[pl.ds(0, USED)], act_out, out_sem.at[0])
 
+    def down_grad():
+        for j in BLOCKS:
+            wg0[j, :] = dot_tn(g[:, j], dy2[...]).astype(BF16)
+        now(0, 0)
+
+    def up_grad():
+        for j in BLOCKS:
+            wg1[j, :] = dot_tn(a2[:, j], dh[...]).astype(BF16)
+        now(1, 0)
+
+    def attention_grads():
+        for k in range(6):
+            i, j = k // 2, BLOCKS[k % 2]
+            part = dot_tn(a1[:, j], dqkv[:, i * W : (i + 1) * W]).astype(BF16)
+            wgs[3 + k // 3][k % 3 * 512 : k % 3 * 512 + 512, :] = part
+            if k % 3 == 2:
+                now(3 + k // 3, 0)
+        wg2[...] = dot_tn(att[...], dy1[...]).astype(BF16)
+        now(2, 0)
+
     def feed_back(h):
         half = HALVES[h]
         for j in BLOCKS:
@@ -465,50 +486,27 @@
         start(ex[DA2, h])
 
     def receive(h):
-        back[h].wait_recv()
-        dy2[mine[h], :] = pipe_b[h]
-        doc[OWN[h], :] = pipe_b[h].astype(F32)
-        start(ex[DOUT, h])
+        arrive(back[h])
+        doc[OWN[h], :] = dy2[mine[h], :].astype(F32)
 
     @pl.when(first)
     def _():
         for h in range(2):
             layer_output(h)
-            forth[h].start()
+            start(forth[h])
             start(ex[OUT, h])
         receive(1)
-        arrive(ex[DOUT, 1])
+        output_grads(1)
+
+    feed_back(1)
+
+    @pl.when(first)
+    def _():
         receive(0)
-        output_grads(1)
-
-    feed_back(1)
-
-    @pl.when(first)
-    def _():
-        arrive(ex[DOUT, 0])
+        down_grad()
         output_grads(0)
 
     feed_back(0)
-
-    def down_grad():
-        for j in BLOCKS:
-            wg0[j, :] = dot_tn(g[:, j], dy2[...]).astype(BF16)
-        now(0, 0)
-
-    def up_grad():
-        for j in BLOCKS:
-            wg1[j, :] = dot_tn(a2[:, j], dh[...]).astype(BF16)
-        now(1, 0)
-
-    def attention_grads():
-        wg2[...] = dot_tn(att[...], dy1[...]).astype(BF16)
-        now(2, 0)
-        for j in range(D // W):
-            part = dot_tn(a1[:, j * W : (j + 1) * W], dqkv[...]).astype(BF16)
-            for i in range(3):
-                at = i * D + j * W
-                wg3[at : at + W, :] = part[:, i * W : (i + 1) * W]
-        now(3, 0)
 
     def middle_back(h):
         arrive(ex[DA2, h])
@@ -523,12 +521,11 @@
         sm[3:4, :] += shift_grad
         sm[4:5, :] += jnp.sum(grad_middle, 0, keepdims=True)
 
-    pl.when(first)(down_grad)
+    pl.when(first)(up_grad)
+    early(0, 1)
     middle_back(1)
-    pl.when(first)(up_grad)
+    early(1, 1)
     middle_back(0)
-    early(0, 1)
-    early(1, 1)
 
     def attend_back(h):
         half, keys = HALVES[h], slice(0, (h + 1) * HALF)
@@ -573,18 +570,21 @@
         )
         low = (dx2c[OWN[h], :] + grad_u).astype(BF16)
         pipe_bs[h] = low
-        pl.when(second)(lambda: back[h].start())
+        pl.when(second)(lambda: start(back[h]))
         dxg[mine[h], :] = low
         start(ex[DX, h])
         sm[0:1, :] += gain_grad
         sm[2:3, :] += shift_grad
 
     attend_back(1)
+    early(0, 2)
     attend_back(0)
-    early(0, 2)
+    early(1, 2)
     pl.when(first)(attention_grads)
-    early(1, 2)
+    early(0, 3)
     input_grads(1)
+    early(3, 1)
+    early(4, 1)
     input_grads(0)
 
     @pl.when(first)
@@ -646,28 +646,32 @@
         dx_copy.start()
 
     if reduce_dp:
+        early(1, 3)
+        early(0, 4)
         early(2, 1)
-        early(3, 1)
 
         @pl.when(second)
         def _():
-            for b, s in ((0, 1), (1, 1), (0, 2), (1, 2), (2, 1), (3, 1)):
+            for b, s in (
+                (0, 1), (1, 1), (0, 2), (1, 2), (3, 1), (4, 1), (2, 1), (0, 3), (1, 3), (0, 4),
+            ):
                 steps[b][s]()
 
         def wave(*items):
             for b, s in items:
                 steps[b][s]()
 
+        wave((3, 2), (4, 2), (1, 4), (2, 2), (0, 5))
         small0()
-        wave((0, 3), (1, 3), (3, 2), (2, 2))
+        wave((3, 3), (4, 3), (2, 3), (1, 5), (0, 6))
         small1()
-        wave((0, 4), (1, 4), (3, 3), (2, 3))
+        wave((3, 4), (4, 4), (2, 4), (1, 6))
         small2()
-        wave((0, 5), (1, 5), (3, 4), (2, 4))
+        wave((3, 5), (4, 5), (2, 5), (0, 7))
         small3()
+        wave((3, 6), (4, 6), (2, 6), (1, 7))
         layer_results()
-        wave((3, 5), (2, 5), (0, 6), (1, 6), (3, 6), (2, 6))
-        wave((0, 7), (1, 7), (3, 7), (2, 7), (0, 8), (1, 8), (3, 8), (2, 8))
+        wave((3, 7), (4, 7), (2, 7), (0, 8), (1, 8), (2, 8), (3, 8), (4, 8))
     else:
         small0()
         layer_results()
@@ -682,18 +686,16 @@
     @pl.when(first)
     def _():
         for h in range(2):
-            forth[h].wait_send()
-            sent(ex[DOUT, h])
+            sent(forth[h])
 
     @pl.when(second)
     def _():
         for h in range(2):
-            back[h].wait_send()
-            sent(ex[A1, h])
+            sent(back[h])
 
     if not reduce_dp:
         copies = [
-            pltpu.make_async_copy(wg, out, dp_l.at[b, 0])
+            pltpu.make_async_copy(wg, out.at[pl.ds(PLACE[b], BUCKETS[b][0])], dp_l.at[b, 0])
             for b, (wg, out) in enumerate(zip(wgs, gouts))
         ]
         start(copies)
@@ -720,7 +722,7 @@
         low(PAD, D), low(2, 3, CH, D), low(PAD, D), wide(2 * CH, D), low(PAD, D), wide(PAD, D), low(PAD, D),
         low(PAD, D), low(2, 3, CH, D), wide(2 * CH, D), low(PAD, D), low(PAD, 768), low(PAD, D),
         low(2, 3, CH, D), low(PAD, D),
-        low(2, CH, D), low(2, CH, D), low(2, CH, D), low(2, CH, D), wide(HALF, W), wide(HALF, W),
+        low(PAD, D), low(2, CH, D), low(2, CH, D), wide(HALF, W), wide(HALF, W),
         wide(8, D), wide(4, 8, D), wide(2, 8, D), wide(2, 8, D), wide(4, 8, D),
     ]
     scratch += [low(size, width) for size, width, _ in BUCKETS]
@@ -731,15 +733,15 @@
     ]
     dma = pltpu.SemaphoreType.DMA
     scratch += [
-        dma((12,)), dma((2,)), dma((22, 3)), dma((22, 3)), dma((4,)), dma((4,)),
-        dma((4, 22)), dma((4, 22)), dma((4, 3)), dma((5,)), dma((5,)),
+        dma((12,)), dma((2,)), dma((18, 3)), dma((18, 3)), dma((4, 4)), dma((4, 4)),
+        dma((5, 22)), dma((5, 22)), dma((5, 3)), dma((5,)), dma((5,)),
     ]
     return pl.pallas_call(
         functools.partial(kernel, reduce_dp),
         out_shape=[
             jax.ShapeDtypeStruct((USED, D), BF16),
             jax.ShapeDtypeStruct((USED, D), BF16),
-            *[jax.ShapeDtypeStruct((size, width), BF16) for size, width, _ in BUCKETS],
+            *[jax.ShapeDtypeStruct(shape, BF16) for shape in ((D, D), (D, D), (W, D), (3 * D, W))],
             jax.ShapeDtypeStruct((8, D), F32),
         ],
         in_specs=[hbm, hbm, smem] + [hbm] * 10,
@@ -754,37 +756,49 @@
 
 def widen_kernel(*refs):
     small, lows = refs[6], refs[:6]
-    outs, (gains, shifts, qv, biases, upb) = refs[7:13], refs[13:]
-    for low, out in zip(lows, outs):
-        out[...] = low[...].astype(F32)
+    outs, (gains, shifts, qv, biases, upb) = refs[7:13], refs[13:18]
+    narrow, wide, (in_sem, out_sem) = refs[18:24], refs[24:30], refs[30:]
+    pieces = []
+    for k in (2, 3, 5, 4, 0, 1):
+        size = lows[k].shape[0]
+        step = ROWS if size == USED else min(size, 128 * D // lows[k].shape[1])
+        for at in range(0, size, step):
+            part, n = pl.ds(at, step), len(pieces)
+            pieces.append((
+                pltpu.make_async_copy(lows[k].at[part], narrow[k].at[part], in_sem.at[n]),
+                pltpu.make_async_copy(wide[k].at[part], outs[k].at[part], out_sem.at[n]),
+                narrow[k].at[part],
+                wide[k].at[part],
+            ))
+    for read, _, _, _ in pieces:
+        read.start()
     gains[...] = small[0:2, :]
     shifts[...] = small[2:4, :]
     biases[...] = small[4:6, :]
     qv[0:1, :] = small[6:7, 0:W]
     qv[1:2, :] = small[6:7, W : 2 * W]
     upb[...] = small[7:8, :]
+    for read, write, source, target in pieces:
+        read.wait()
+        target[...] = source[...].astype(F32)
+        write.start()
+    for _, write, _, _ in pieces:
+        write.wait()
 
 
 def widen(lows, small):
-    count = 8
-
-    def spec(shape):
-        blocks = 5 if shape[0] == USED else count
-        return pl.BlockSpec(
-            (shape[0] // blocks, shape[1]), lambda i: (jnp.minimum(i, blocks - 1), 0)
-        )
-
-    def fixed(shape):
-        return pl.BlockSpec(shape, lambda i: (0, 0))
-
+    hbm = pl.BlockSpec(memory_space=pltpu.HBM)
+    vmem = pl.BlockSpec(memory_space=pltpu.VMEM)
     flat = [(2, D), (2, D), (2, W), (2, D), (1, D)]
     return pl.pallas_call(
         widen_kernel,
-        grid=(count,),
         out_shape=[jax.ShapeDtypeStruct(a.shape, F32) for a in lows]
         + [jax.ShapeDtypeStruct(shape, F32) for shape in flat],
-        in_specs=[spec(a.shape) for a in lows] + [fixed((8, D))],
-        out_specs=[spec(a.shape) for a in lows] + [fixed(shape) for shape in flat],
+        in_specs=[hbm] * 6 + [vmem],
+        out_specs=[hbm] * 6 + [vmem] * 5,
+        scratch_shapes=[pltpu.VMEM(a.shape, BF16) for a in lows]
+        + [pltpu.VMEM(a.shape, F32) for a in lows]
+        + [pltpu.SemaphoreType.DMA((32,)), pltpu.SemaphoreType.DMA((32,))],
         compiler_params=pltpu.CompilerParams(vmem_limit_bytes=60 * 1024 * 1024),
         name="widen",
     )(*lows, small)

time: 165 us -> 153 us (0.927)
  Pallas kernels: 164 us -> 152 us
    pallas_call x1, Pallas kernels: 155 us -> 144 us  [call(): pl.pallas_call(functools.partial(kernel, reduce_dp), out_shape=[jax.Shape...]
where the time goes in v5:
time: 153 us
  Pallas kernels  152 us (99%)
    pallas_call x1, Pallas kernels, call(): pl.pallas_call(functools.partial(kernel, reduce_dp), out_shape=[jax.Shape...  144 us
    pallas_call x1, Pallas kernels, widen(): pl.pallas_call(widen_kernel, out_shape=[jax.ShapeDtypeStruct(a.shape, F32...  8.84 us

profile of v5, /device:TPU:1, one launch (start us, length us, event | category | flops | bytes accessed | tf_op | source)
XLA Modules:
  0.0 153.3 jit_solution(7476918505871454441)
XLA Ops:
  0.6 143.6 %layers.1 = (bf16[240,1024]{1,0:T(8,128)(2,1)}, bf16[240,1024]{1,0:T(8,128)(2,1)}, bf16[1024,1024]{1,0:T(8,128)(2,1)}, bf16[1024,1024]{1,0:T(8,128)(2,1)}, bf16[...) custom-call(f32[240,1024]{1,0:T(8,128)} %bitcast.29, f32[240,1024]{1,0:T(8,128)} %bitcast.30, ...), custom_call_target="tpu_custom_call" | custom-call | tf_op jit(solution)/shard_map/layers/pallas_call | solution.py:739
  144.3 8.8 %widen.1 = (f32[240,1024]{1,0:T(8,128)}, f32[240,1024]{1,0:T(8,128)}, f32[1024,1024]{1,0:T(8,128)}, f32[1024,1024]{1,0:T(8,128)}, f32[256,1024]{1,0:T(8,128)}, /...) custom-call(bf16[240,1024]{1,0:T(8,128)(2,1)} %get-tuple-element.29., ...), custom_call_target="tpu_custom_call" | custom-call | tf_op jit(solution)/shard_map/widen/pallas_call | solution.py:793

commit v6 on v5

--- a/solution.py
+++ b/solution.py
@@ -73,7 +73,7 @@
     act_out, dx_out, gdn_out, gup_out, go_out, gqkv_out, small_out,
     tok, cot, wqkv, wo, wup, wdn, mask, xc, a1, qkv, prob, att, y1s, y1r, x2c, a2, slope, g,
     y2s, y2r, actg, doc, dy2, dg, dh, da2s, da2r, dx2c, dy1, dqkv, da1s, da1r, dxg,
-    pipe_f, pipe_fs, pipe_bs, kacc, vacc, sm, smz, smc, smy, smx,
+    pipe_f, pipe_fs, pipe_bs, kacc, vacc, smo, sm, smz, smc, smy, smx,
     wg0, wg1, wg2, wg3, wg4, rc0, rc1, rc2, rc3, rc4, in0, in1, in2, in3, in4,
     live, gains, shifts, qvb, obias, upb,
     load_sem, out_sem, tp_s, tp_r, pp_s, pp_r, dp_s, dp_r, dp_l, sd_s, sd_r,
@@ -524,8 +524,8 @@
     pl.when(first)(up_grad)
     early(0, 1)
     middle_back(1)
+    middle_back(0)
     early(1, 1)
-    middle_back(0)
 
     def attend_back(h):
         half, keys = HALVES[h], slice(0, (h + 1) * HALF)
@@ -610,6 +610,8 @@
         y_copy = sd_copy(1, smy.at[gy], smy.at[gy], y_peer)
         x_copies = [sd_copy(2 + i, smx.at[gx], smx.at[gx], x_peers[i]) for i in range(3)]
 
+    small_copy = pltpu.make_async_copy(smo, small_out, out_sem.at[2])
+
     def small0():
         arrive(ex[SMALL, 0])
         whole = smz[0] + smz[1] + smz[2] + smz[3]
@@ -619,7 +621,8 @@
             smc[gc] = whole
             core_copy.start()
         else:
-            small_out[...] = whole
+            smo[...] = whole
+            small_copy.start()
 
     def small1():
         core_copy.wait()
@@ -634,7 +637,8 @@
     def small3():
         for copy in x_copies:
             copy.wait()
-        small_out[...] = smx[0] + smx[1] + smx[2] + smx[3]
+        smo[...] = smx[0] + smx[1] + smx[2] + smx[3]
+        small_copy.start()
 
     dx_copy = pltpu.make_async_copy(dxg.at[pl.ds(0, USED)], dx_out, out_sem.at[1])
 
@@ -678,6 +682,7 @@
 
     act_copy.wait()
     dx_copy.wait()
+    small_copy.wait()
     sent(ex[SMALL, 0])
     for h in range(2):
         for k in (Y1, A2, Y2, OUT, DA2, DY1, DA1, DX):
@@ -706,7 +711,6 @@
 def call(reduce_dp, *operands):
     hbm = pl.BlockSpec(memory_space=pltpu.HBM)
     anywhere = pl.BlockSpec(memory_space=pl.ANY)
-    vmem = pl.BlockSpec(memory_space=pltpu.VMEM)
     smem = pl.BlockSpec(memory_space=pltpu.SMEM)
 
     def low(*shape):
@@ -723,6 +727,7 @@
         low(PAD, D), low(2, 3, CH, D), wide(2 * CH, D), low(PAD, D), low(PAD, 768), low(PAD, D),
         low(2, 3, CH, D), low(PAD, D),
         low(PAD, D), low(2, CH, D), low(2, CH, D), wide(HALF, W), wide(HALF, W),
+        wide(8, D),
         wide(8, D), wide(4, 8, D), wide(2, 8, D), wide(2, 8, D), wide(4, 8, D),
     ]
     scratch += [low(size, width) for size, width, _ in BUCKETS]
@@ -733,7 +738,7 @@
     ]
     dma = pltpu.SemaphoreType.DMA
     scratch += [
-        dma((12,)), dma((2,)), dma((18, 3)), dma((18, 3)), dma((4, 4)), dma((4, 4)),
+        dma((12,)), dma((3,)), dma((18, 3)), dma((18, 3)), dma((4, 4)), dma((4, 4)),
         dma((5, 22)), dma((5, 22)), dma((5, 3)), dma((5,)), dma((5,)),
     ]
     return pl.pallas_call(
@@ -745,7 +750,7 @@
             jax.ShapeDtypeStruct((8, D), F32),
         ],
         in_specs=[hbm, hbm, smem] + [hbm] * 10,
-        out_specs=[anywhere] * 6 + [vmem],
+        out_specs=[anywhere] * 7,
         scratch_shapes=scratch,
         compiler_params=pltpu.CompilerParams(
             collective_id=0, has_side_effects=True, vmem_limit_bytes=60 * 1024 * 1024
@@ -755,9 +760,12 @@
 
 
 def widen_kernel(*refs):
-    small, lows = refs[6], refs[:6]
-    outs, (gains, shifts, qv, biases, upb) = refs[7:13], refs[13:18]
-    narrow, wide, (in_sem, out_sem) = refs[18:24], refs[24:30], refs[30:]
+    small_in, lows = refs[6], refs[:6]
+    outs, flat = refs[7:13], refs[13:18]
+    narrow, wide = refs[18:24], refs[24:30]
+    small, (gains, shifts, qv, biases, upb), (in_sem, out_sem) = refs[30], refs[31:36], refs[36:]
+    first = pltpu.make_async_copy(small_in, small, in_sem.at[32])
+    first.start()
     pieces = []
     for k in (2, 3, 5, 4, 0, 1):
         size = lows[k].shape[0]
@@ -772,33 +780,43 @@
             ))
     for read, _, _, _ in pieces:
         read.start()
+    first.wait()
     gains[...] = small[0:2, :]
     shifts[...] = small[2:4, :]
     biases[...] = small[4:6, :]
     qv[0:1, :] = small[6:7, 0:W]
     qv[1:2, :] = small[6:7, W : 2 * W]
     upb[...] = small[7:8, :]
+    last = [
+        pltpu.make_async_copy(source, out, out_sem.at[32 + n])
+        for n, (source, out) in enumerate(zip((gains, shifts, qv, biases, upb), flat))
+    ]
+    for copy in last:
+        copy.start()
     for read, write, source, target in pieces:
         read.wait()
         target[...] = source[...].astype(F32)
         write.start()
     for _, write, _, _ in pieces:
         write.wait()
+    for copy in last:
+        copy.wait()
 
 
 def widen(lows, small):
     hbm = pl.BlockSpec(memory_space=pltpu.HBM)
-    vmem = pl.BlockSpec(memory_space=pltpu.VMEM)
     flat = [(2, D), (2, D), (2, W), (2, D), (1, D)]
     return pl.pallas_call(
         widen_kernel,
         out_shape=[jax.ShapeDtypeStruct(a.shape, F32) for a in lows]
         + [jax.ShapeDtypeStruct(shape, F32) for shape in flat],
-        in_specs=[hbm] * 6 + [vmem],
-        out_specs=[hbm] * 6 + [vmem] * 5,
+        in_specs=[hbm] * 7,
+        out_specs=[hbm] * 11,
         scratch_shapes=[pltpu.VMEM(a.shape, BF16) for a in lows]
         + [pltpu.VMEM(a.shape, F32) for a in lows]
-        + [pltpu.SemaphoreType.DMA((32,)), pltpu.SemaphoreType.DMA((32,))],
+        + [pltpu.VMEM((8, D), F32)]
+        + [pltpu.VMEM(shape, F32) for shape in flat]
+        + [pltpu.SemaphoreType.DMA((33,)), pltpu.SemaphoreType.DMA((37,))],
         compiler_params=pltpu.CompilerParams(vmem_limit_bytes=60 * 1024 * 1024),
         name="widen",
     )(*lows, small)

time: 153 us -> 152 us (level)
  no operation moved by 1% of the time
where the time goes in v6:
time: 152 us; the launch traced here: 151 us
  Pallas kernels  151 us (99%)
    pallas_call x1, Pallas kernels, call(): pl.pallas_call(functools.partial(kernel, reduce_dp), out_shape=[jax.Shape...  143 us
    pallas_call x1, Pallas kernels, widen(): pl.pallas_call(widen_kernel, out_shape=[jax.ShapeDtypeStruct(a.shape, F32...  7.57 us

profile of v6, /device:TPU:1, one launch (start us, length us, event | category | flops | bytes accessed | tf_op | source)
XLA Modules:
  0.0 151.5 jit_solution(14255380323332422945)
XLA Ops:
  0.6 143.1 %layers.1 = (bf16[240,1024]{1,0:T(8,128)(2,1)}, bf16[240,1024]{1,0:T(8,128)(2,1)}, bf16[1024,1024]{1,0:T(8,128)(2,1)}, bf16[1024,1024]{1,0:T(8,128)(2,1)}, bf16[...) custom-call(f32[240,1024]{1,0:T(8,128)} %bitcast.29, f32[240,1024]{1,0:T(8,128)} %bitcast.30, ...), custom_call_target="tpu_custom_call" | custom-call | tf_op jit(solution)/shard_map/layers/pallas_call | solution.py:744
  143.7 7.6 %widen.1 = (f32[240,1024]{1,0:T(8,128)}, f32[240,1024]{1,0:T(8,128)}, f32[1024,1024]{1,0:T(8,128)}, f32[1024,1024]{1,0:T(8,128)}, f32[256,1024]{1,0:T(8,128)}, /...) custom-call(bf16[240,1024]{1,0:T(8,128)(2,1)} %get-tuple-element.29., ...), custom_call_target="tpu_custom_call" | custom-call | tf_op jit(solution)/shard_map/widen/pallas_call | solution.py:809
